TPU v7x, 32 devices: a whole 2x2x4 slice. The times are simulated.
32 devices in a mesh: grp: 4 (over z), rep: 8 (over y, x, core).
Axes of the slice: x: 2, y: 2, z: 4, core: 2. Of those that a mesh axis runs over, the one named last changes fastest.
Arguments:
- tokens: bfloat16 [64, 512, 768], P(('grp', 'rep')), may hold values from -6 to 6
- lengths: int32 [64], P(('grp', 'rep')), may hold values from 1 to 512, 19660 in all
- cotangent: bfloat16 [64, 512, 768], P(('grp', 'rep')), may hold values from -6 to 6
- query_weight: bfloat16 [768, 768], P('grp'), may hold values from -0.21875 to 0.21875
- query_bias: bfloat16 [768], P('grp'), may hold values from -1.75 to 1.75
- key_weight: bfloat16 [768, 768], P('grp'), may hold values from -0.21875 to 0.21875
- value_weight: bfloat16 [768, 768], P('grp'), may hold values from -0.21875 to 0.21875
- value_bias: bfloat16 [768], P('grp'), may hold values from -1.75 to 1.75
- out_weight: bfloat16 [768, 768], P('grp'), may hold values from -1.75 to 1.75
- out_bias: bfloat16 [768], P('grp'), may hold values from -1.75 to 1.75
- norm_gain: bfloat16 [768], P('grp'), may hold values from 0.5 to 1.5
- norm_shift: bfloat16 [768], P('grp'), may hold values from -1.75 to 1.75
- up_weight: bfloat16 [768, 3072], P('grp'), may hold values from -0.21875 to 0.21875
- up_bias: bfloat16 [3072], P('grp'), may hold values from -3 to 3
- down_weight: bfloat16 [3072, 768], P('grp'), may hold values from -0.109375 to 0.109375
- down_bias: bfloat16 [768], P('grp'), may hold values from -1.75 to 1.75
- final_gain: bfloat16 [768], P('grp'), may hold values from 0.5 to 1.5
- final_shift: bfloat16 [768], P('grp'), may hold values from -1.75 to 1.75
Outputs:
- output: bfloat16 [64, 512, 768], P(('grp', 'rep'))
- grad_tokens: bfloat16 [64, 512, 768], P(('grp', 'rep'))
- grad_query_weight: float32 [768, 768], P('grp')
- grad_query_bias: float32 [768], P('grp')
- grad_key_weight: float32 [768, 768], P('grp')
- grad_value_weight: float32 [768, 768], P('grp')
- grad_value_bias: float32 [768], P('grp')
- grad_out_weight: float32 [768, 768], P('grp')
- grad_out_bias: float32 [768], P('grp')
- grad_norm_gain: float32 [768], P('grp')
- grad_norm_shift: float32 [768], P('grp')
- grad_up_weight: float32 [768, 3072], P('grp')
- grad_up_bias: float32 [3072], P('grp')
- grad_down_weight: float32 [3072, 768], P('grp')
- grad_down_bias: float32 [768], P('grp')
- grad_final_gain: float32 [768], P('grp')
- grad_final_shift: float32 [768], P('grp')
Inputs may be any that keep to these rules, and one draw needn't show every extreme that they name: Every pair has at least one token; slots from lengths on are padding.
All inputs are finite; a program needn't handle non-finite values. No bound on the sum of `lengths` on one device may be relied on, other than what follows from the above.
Results may differ from a plain program's by a relative error of at most 0.017.
Values may be sent and summed in bfloat16 or wider, within the bound.
No kernel may reach another device: no remote copies, remote signals or barrier semaphores. Data moves between devices by JAX's collectives and lax.ppermute only.
A program may use at most 192 MiB of HBM per device.

v0:
```python
import functools

import jax
import jax.numpy as jnp
from jax import lax
from jax.experimental import pallas as pl
from jax.experimental.pallas import tpu as pltpu
from jax.sharding import PartitionSpec as P

H = 12
HD = 64
EPSILON = 1e-06
MASKED = -1e30
DENSITY = 0.3989422804014327
ROOT_HALF = 0.7071067811865476

f32 = jnp.float32
bf16 = jnp.bfloat16
VMEM = pl.BlockSpec(memory_space=pltpu.VMEM)
SMEM = pl.BlockSpec(memory_space=pltpu.SMEM)
ANY = pl.BlockSpec(memory_space=pl.ANY)
VMEM_LIMIT = 56 * 2**20
COLS = 384
WEIGHT = 20
LOCAL = 8


def dot(a, b):
    return jnp.dot(a, b, preferred_element_type=f32)


def nt(a, b):
    return lax.dot_general(a, b, (((1,), (1,)), ((), ())), preferred_element_type=f32)


def tn(a, b):
    return lax.dot_general(a, b, (((0,), (0,)), ((), ())), preferred_element_type=f32)


def shape(dims, dtype):
    return jax.ShapeDtypeStruct(dims, dtype)


def al(value, by):
    return pl.multiple_of(value, by)


def call(kernel, outs, args, specs, out_specs, scratch=(), grid=(), flops=0, moved=0, aliases=None, **fixed):
    return pl.pallas_call(
        functools.partial(kernel, **fixed) if fixed else kernel,
        grid=grid,
        out_shape=outs,
        in_specs=specs,
        out_specs=out_specs,
        scratch_shapes=scratch,
        input_output_aliases=aliases or {},
        compiler_params=pltpu.CompilerParams(vmem_limit_bytes=VMEM_LIMIT),
        cost_estimate=pl.CostEstimate(
            flops=WEIGHT * flops, bytes_accessed=WEIGHT * moved, transcendentals=0
        ),
        name=kernel.__name__,
    )(*args)


def after(values, *events):
    return lax.optimization_barrier((values, events))[0]


def to_rep(array, bit):
    size = lax.axis_size("rep")
    return lax.ppermute(array, "rep", [(i, i ^ bit) for i in range(size)])


def to_grp(array, bit):
    size = lax.axis_size("grp")
    return lax.ppermute(array, "grp", [(i, i ^ bit) for i in range(size)])


def position():
    z = lax.axis_index("grp").astype(jnp.int32)
    p = lax.axis_index("rep").astype(jnp.int32) % LOCAL
    return jnp.stack([z, (p // 2) % 2, p // 4, p % 2, p])


class Copies:
    def __init__(self, sems):
        self.sems, self.held = sems, []

    def add(self, src, dst):
        copy = pltpu.make_async_copy(src, dst, self.sems.at[len(self.held)])
        copy.start()
        self.held.append(copy)

    def wait(self):
        for copy in self.held:
            copy.wait()


def piece_refs(kind, ref, zone, p, depth):
    if kind == "tall":
        rows = depth // LOCAL
        start = al(zone * depth + p * rows, 16)
        return [
            (ref.at[pl.ds(start, rows), pl.ds(half * COLS, COLS)], rows) for half in range(2)
        ]
    if kind == "wide":
        rows = depth // 2
        start = al(zone * depth + (p % 2) * rows, 16)
        return [
            (
                ref.at[pl.ds(start, rows), pl.ds(al((p // 2) * 2 * COLS + half * COLS, 128), COLS)],
                rows,
            )
            for half in range(2)
        ]
    if kind == "half":
        rows = depth // 2
        start = al(zone * depth + (p % 2) * rows, 16)
        return [(ref.at[pl.ds(start, rows), pl.ds(al((p // 2) * COLS, 128), COLS)], rows)]
    rows = depth // 4
    offset = int(kind)
    start = al(zone * depth + (p // 2) * rows, 16)
    return [(ref.at[pl.ds(start, rows), pl.ds(al(offset + (p % 2) * COLS, 128), COLS)], rows)]


def own_slab(ref, zone, depth, first=0, width=None):
    width = ref.shape[1] if width is None else width
    return ref.at[pl.ds(al(zone * depth, 16), depth), pl.ds(first, width)]


def block_rows(parts):
    return sum(rows for kind, ref, depth in parts for _, rows in piece_refs(kind, ref, 0, 0, depth))


def fetch(copies, pos, parts, held):
    zone, p = pos[0], pos[4]
    groups = lax.axis_size("grp")
    n = held[0].shape[0] // (groups - 1)
    side = len(held) // 2
    for sib in range(2):
        for other in range(4):
            owner = p ^ (other * 2) ^ sib
            part = held[side * sib + other]
            cut = part.shape[0]
            for step in range(1, groups):
                source = zone ^ step
                at = (step - 1) * n
                for kind, ref, depth in parts:
                    for place, rows in piece_refs(kind, ref, source, owner, depth):
                        first = max(0, min(cut - at, rows))
                        if first:
                            copies.add(part.at[pl.ds(at, first), :], place.at[pl.ds(0, first), :])
                        if first < rows:
                            copies.add(
                                held[side * sib + 4].at[pl.ds(at + first - cut, rows - first), :],
                                place.at[pl.ds(first, rows - first), :],
                            )
                        at += rows


def emit(copies, pos, parts, send, keep, quads=range(4)):
    core = pos[3]
    groups = lax.axis_size("grp")
    for held, flip in ((send, 1), (keep, 0)):
        for zone in range(groups):
            for q in quads:
                owner = q * 2 + (core ^ flip)
                at = 0
                for kind, ref, depth in parts:
                    for place, rows in piece_refs(kind, ref, zone, owner, depth):
                        copies.add(place, held.at[zone, q, pl.ds(at, rows), :])
                        at += rows


def add_first(pos, keep, got, sa, ka, sb, kb):
    x, y = pos[1], pos[2]
    half = keep.shape[0] // 2
    for zone in range(half):
        for j in range(2):
            for ref, q in ((sa, j * 2 + (1 - x)), (ka, j * 2 + x)):
                ref[zone, j] = keep[zone, q] + got[zone, q]
            for ref, q in ((sb, (1 - y) * 2 + j), (kb, y * 2 + j)):
                ref[zone, j] = keep[half + zone, q] + got[half + zone, q]


def add_second(pos, ka, ra, kb, rb, sa, ja, sb, jb):
    x, y = pos[1], pos[2]
    for zone in range(ka.shape[0]):
        for kept, got, send, hold, at in ((ka, ra, sa, ja, y), (kb, rb, sb, jb, x)):
            send[zone] = kept[zone, 1 - at] + got[zone, 1 - at]
            hold[zone] = kept[zone, at] + got[zone, at]


def add_third(pos, ka, ra, kb, rb, *rest):
    outs, total = rest[:-1], rest[-1]
    half = ka.shape[0]
    for zone in range(half):
        total[zone] = ka[zone] + ra[zone]
        total[half + zone] = kb[zone] + rb[zone]
    for step, out in enumerate(outs):
        out[...] = total[pos[0] ^ step]


def add_direct(pos, keep, got, *outs):
    q = pos[2] * 2 + pos[1]
    for zone in range(keep.shape[0]):
        for i, out in enumerate(outs):
            out[zone] = keep[zone, q ^ i] + got[zone, q ^ i]


def add_third_with(pos, ka, ra, kb, rb, mine, a, b, c, *rest):
    outs, total = rest[:-1], rest[-1]
    half, n = ka.shape[:2]
    for zone in range(half):
        total[zone, :n] = ka[zone] + ra[zone]
        total[half + zone, :n] = kb[zone] + rb[zone]
    for zone in range(2 * half):
        sums = mine[zone].astype(f32) + a[zone].astype(f32)
        total[zone, n:] = (sums + (b[zone].astype(f32) + c[zone].astype(f32))).astype(bf16)
    for step, out in enumerate(outs):
        out[...] = total[pos[0] ^ step]


def add_zones(ka, ra, kb, rb, other, out):
    half, n = ka.shape[0], other.shape[1]
    out[:, :n] = other[...]
    out[:half, n:] = ka[...] + ra[...]
    out[half:, n:] = kb[...] + rb[...]


def add_fourth(*refs):
    total = refs[0][...].astype(f32)
    for ref in refs[1:-1]:
        total = total + ref[...].astype(f32)
    refs[-1][...] = total.astype(bf16)


def over_blocks(total):
    bit = LOCAL
    while bit < lax.axis_size("rep"):
        other = to_rep(total, bit)
        total = call(add_fourth, shape(total.shape, bf16), (total, other), [VMEM] * 2, VMEM)
        bit *= 2
    return total


class Reduce:
    def __init__(self, pos, send, keep):
        self.pos, self.keep = pos, keep
        self.n = keep.shape[2]
        self.size = keep.shape[0] * 4 * self.n * COLS * 2
        self.got = to_rep(send, 1)

    def one(self, *events):
        groups = self.keep.shape[0]
        quad = shape((groups // 2, 2, self.n, COLS), bf16)
        got = after(self.got, *events)
        sa, self.ka, sb, self.kb = call(
            add_first,
            (quad,) * 4,
            (self.pos, self.keep, got),
            [SMEM, VMEM, VMEM],
            (VMEM,) * 4,
            moved=3 * self.size,
        )
        self.ra, self.rb = to_rep(sa, 2), to_rep(sb, 4)
        return self.ka

    def two(self, *events):
        pair = shape((self.ka.shape[0], self.n, COLS), bf16)
        ra, rb = after((self.ra, self.rb), *events)
        sa, self.ja, sb, self.jb = call(
            add_second,
            (pair,) * 4,
            (self.pos, self.ka, ra, self.kb, rb),
            [SMEM] + [VMEM] * 4,
            (VMEM,) * 4,
            moved=3 * self.size // 2,
        )
        self.ra, self.rb = to_rep(sa, 4), to_rep(sb, 2)
        return self.ja

    def zones(self, other, *events):
        ra, rb = after((self.ra, self.rb), *events)
        groups, n, _ = other.shape
        return call(
            add_zones,
            shape((groups, n + self.n, COLS), bf16),
            (self.ja, ra, self.jb, rb, other),
            [VMEM] * 5,
            VMEM,
            moved=3 * self.size // 4,
        )

    def three(self, *events):
        groups = self.keep.shape[0]
        ra, rb = after((self.ra, self.rb), *events)
        self.blocks = call(
            add_third,
            (shape((self.n, COLS), bf16),) * groups,
            (self.pos, self.ja, ra, self.jb, rb),
            [SMEM] + [VMEM] * 4,
            (VMEM,) * groups,
            scratch=[pltpu.VMEM((groups, self.n, COLS), bf16)],
            moved=3 * self.size // 4,
        )
        self.arrived = [to_grp(self.blocks[step], step) for step in range(1, groups)]
        return self.blocks[0]

    def direct(self, *events):
        groups = self.keep.shape[0]
        got = after(self.got, *events)
        self.mine, *sends = call(
            add_direct,
            (shape((groups, self.n, COLS), bf16),) * 4,
            (self.pos, self.keep, got),
            [SMEM, VMEM, VMEM],
            (VMEM,) * 4,
            moved=3 * self.size,
        )
        self.near = [to_rep(send, 2 * (i + 1)) for i, send in enumerate(sends)]
        return self.mine

    def three_with(self, small, *events):
        groups = self.keep.shape[0]
        ra, rb, near = after((self.ra, self.rb, small.near), *events)
        self.n += small.n
        self.blocks = call(
            add_third_with,
            (shape((self.n, COLS), bf16),) * groups,
            (self.pos, self.ja, ra, self.jb, rb, small.mine, *near),
            [SMEM] + [VMEM] * 8,
            (VMEM,) * groups,
            scratch=[pltpu.VMEM((groups, self.n, COLS), bf16)],
            moved=self.size,
        )
        self.arrived = [to_grp(self.blocks[step], step) for step in range(1, groups)]
        return self.blocks[0]

    def four(self, *events):
        arrived = after(self.arrived, *events)
        one = shape((self.n, COLS), bf16)
        total = call(
            add_fourth,
            one,
            (self.blocks[0], *arrived),
            [VMEM] * (1 + len(arrived)),
            VMEM,
            moved=self.size // 3,
        )
        self.total = over_blocks(total)
        return self.total

    def around(self):
        self.near = [to_rep(self.total, bit) for bit in (2, 4, 6)]

    def five(self, *events):
        near = after(self.near, *events)
        held = jnp.concatenate([self.total, *near], axis=0)
        self.both = held, to_rep(held, 1)
        return held


def cut_first(pos, wq, wk, wv, first):
    quarter = wq.shape[0]
    for m, ref in enumerate((wq, wk, wv)):
        first[m * quarter : (m + 1) * quarter, :] = ref[...]


def cut_more(pos, wo, wu, wd, small, second, third):
    half, quarter = wu.shape[0], wo.shape[0]
    for j in range(2):
        second[j * half : (j + 1) * half, :] = wu[:, j * COLS : (j + 1) * COLS]
        third[j * half : (j + 1) * half, :] = wd[:, j * COLS : (j + 1) * COLS]
    second[2 * half : 2 * half + quarter, :] = wo[...]
    second[2 * half + quarter :, :] = small[...]


def layer_norm(values):
    centred = values - jnp.mean(values, axis=-1, keepdims=True)
    spread_of = jnp.mean(centred * centred, axis=-1, keepdims=True)
    inverse = lax.rsqrt(spread_of + EPSILON)
    return centred * inverse, inverse


def norm_back(upstream, normed, inverse, gain):
    scaled = upstream * gain
    return inverse * (
        scaled
        - jnp.mean(scaled, axis=-1, keepdims=True)
        - normed * jnp.mean(scaled * normed, axis=-1, keepdims=True)
    )


def attend_heads(lengths, x, vectors, weight, q_out, k_out, v_out, mixed, logsum, pair):
    width = x.shape[1]
    rows = x[...]
    scaling = HD ** (-0.5)
    q_out[...] = (
        (dot(rows, weight[:, :width]) + vectors[0:1, :]).astype(bf16).astype(f32) * scaling
    ).astype(bf16)
    k_out[...] = dot(rows, weight[:, width : 2 * width]).astype(bf16)
    v_out[...] = (dot(rows, weight[:, 2 * width :]) + vectors[1:2, :]).astype(bf16)
    slots = rows.shape[0]
    lane = lax.broadcasted_iota(jnp.int32, (slots, 128), 1)
    low = lane < HD
    slot = lax.broadcasted_iota(jnp.int32, (1, slots), 1)
    bias = jnp.where(slot < lengths[pair], 0.0, MASKED).astype(f32)

    def heads(h, sums):
        s = pl.ds(al(h * 128, 128), 128)
        q1, k1, v1 = q_out[:, s], k_out[:, s], v_out[:, s]
        results, peaks = [], []
        for e in range(2):
            mask = low if e == 0 else ~low
            scores = nt(jnp.where(mask, q1, 0).astype(bf16), k1) + bias
            peak = jnp.max(scores, axis=1, keepdims=True)
            expo = jnp.exp(scores - peak).astype(bf16)
            results.append(dot(expo, jnp.where(mask, v1, 1).astype(bf16)))
            peaks.append(peak)
        total = pltpu.roll(jnp.where(low, results[1], results[0]), HD, 1)
        mixed[:, s] = (jnp.where(low, results[0], results[1]) / total).astype(bf16)
        sums = jnp.where(lane % HD == h, jnp.where(low, peaks[0], peaks[1]) + jnp.log(total), sums)
        return sums

    sums = lax.fori_loop(0, H // 2, heads, jnp.zeros((slots, 128), f32), unroll=True)
    turned = sums.T
    logsum[0, :8] = turned[:8]
    logsum[0, 8:] = turned[HD : HD + 8]


def attend(pos, lengths, x, wq, wk, wv, vectors, *rest):
    held, (q_out, k_out, v_out, mixed, logsum, w_out, weight, sems) = rest[:10], rest[10:]
    depth, width = wq.shape
    pair = pl.program_id(0)
    write = pltpu.make_async_copy(weight, w_out, sems.at[sems.shape[0] - 1])

    @pl.when(pair == 0)
    def _():
        copies = Copies(sems)
        for m, ref in enumerate((wq, wk, wv)):
            copies.add(ref, own_slab(weight, pos[0], depth, m * width, width))
        fetch(copies, pos, [(str(m * width), weight, depth) for m in range(3)], held)
        copies.wait()
        write.start()

    attend_heads(lengths, x, vectors, weight, q_out, k_out, v_out, mixed, logsum, pair)

    @pl.when(pair == pl.num_programs(0) - 1)
    def _():
        write.wait()


def expand_rows(x, mixed, vectors, up_bias, up, out_w, act, slope, normed, inverse):
    first = x[...].astype(f32) + dot(mixed[...], out_w[...]) + vectors[2:3, :]
    normal, scale = layer_norm(first)
    normed[...] = normal
    inverse[...] = jnp.broadcast_to(scale, inverse.shape)
    hidden = (normal * vectors[3:4, :] + vectors[4:5, :]).astype(bf16)
    chunk = 768
    for j in range(up.shape[1] // chunk):
        s = slice(j * chunk, (j + 1) * chunk)
        u = dot(hidden, up[:, s]) + up_bias[:, s]
        cdf, pdf = gaussian(u)
        act[:, s] = (u * cdf).astype(bf16)
        slope[:, s] = (cdf + u * pdf).astype(bf16)


def expand(pos, x, mixed, wu, wo, vectors, up_bias, *rest):
    held, (act, slope, normed, inverse, wu_out, wo_out, up, out_w, sems) = rest[:8], rest[8:]
    step = pl.program_id(0)
    depth = wo.shape[0]
    last = sems.shape[0]
    writes = [
        pltpu.make_async_copy(up, wu_out, sems.at[last - 1]),
        pltpu.make_async_copy(out_w, wo_out, sems.at[last - 2]),
    ]

    @pl.when(step == 0)
    def _():
        copies = Copies(sems)
        copies.add(wu, own_slab(up, pos[0], depth))
        copies.add(wo, own_slab(out_w, pos[0], depth))
        fetch(copies, pos, [("wide", up, depth), ("0", out_w, depth)], held)
        copies.wait()
        for write in writes:
            write.start()

    expand_rows(x, mixed, vectors, up_bias, up, out_w, act, slope, normed, inverse)

    @pl.when(step == pl.num_programs(0) - 1)
    def _():
        for write in writes:
            write.wait()


def gaussian(u):
    return 0.5 + 0.5 * lax.erf(u * ROOT_HALF), jnp.exp(-0.5 * u * u) * DENSITY


def contract(pos, lengths, act, normed, cotangent, wd, vectors, *rest):
    held, rest = rest[:8], rest[8:]
    output, grad_second, send, sums, wd_out, down, acts, lows, grads, sems, act_sems, out_sems = rest
    step = pl.program_id(0)
    blocks = pl.num_programs(0) - 1
    depth = wd.shape[0]
    rows = normed.shape[0]
    write = pltpu.make_async_copy(down, wd_out, sems.at[sems.shape[0] - 1])

    def part(i):
        return pltpu.make_async_copy(
            act.at[pl.ds(al(i * rows, 16), rows), :],
            acts.at[pl.ds(al(i * rows, 16), rows), :],
            act_sems.at[i],
        )

    @pl.when(step == 0)
    def _():
        copies = Copies(sems)
        copies.add(wd, own_slab(down, pos[0], depth))
        fetch(copies, pos, [("tall", down, depth)], held)
        for i in range(act_sems.shape[0]):
            part(i).start()
        copies.wait()
        write.start()
        sums[...] = jnp.zeros_like(sums)

    @pl.when(step < blocks)
    def _():
        part(step).wait()
        s = pl.ds(al(step * rows, 16), rows)
        per_pair = acts.shape[0] // lengths.shape[0] // rows
        slot = lax.broadcasted_iota(jnp.int32, (rows, 1), 0) + lax.rem(step, per_pair) * rows
        mask = (slot < lengths[step // per_pair]).astype(f32)
        hidden = normed[...] * vectors[3:4, :] + vectors[4:5, :]
        second = hidden + dot(acts[s, :], down[...]) + vectors[5:6, :]
        normal, scale = layer_norm(second)
        gain = vectors[6:7, :]
        output[...] = ((normal * gain + vectors[7:8, :]) * mask).astype(bf16)
        upstream = cotangent[...].astype(f32) * mask
        result = norm_back(upstream, normal, scale, gain)
        grad_second[...] = result
        low = result.astype(bf16)
        lows[s, :] = low
        sums[0:1, :] += jnp.sum(upstream * normal, axis=0, keepdims=True)
        sums[1:2, :] += jnp.sum(upstream, axis=0, keepdims=True)
        sums[2:3, :] += jnp.sum(low.astype(f32), axis=0, keepdims=True)

    @pl.when(step == blocks)
    def _():
        copies = Copies(out_sems)
        for zone in range(grads.shape[0] // depth):
            s = slice(zone * depth, (zone + 1) * depth)
            grads[s, :] = tn(acts[:, s], lows[...]).astype(bf16)
            for p in range(LOCAL):
                at = 0
                for place, rows in piece_refs("tall", grads, zone, p, depth):
                    copies.add(place, send.at[p, zone, pl.ds(at, rows), :])
                    at += rows
        copies.wait()
        write.wait()


def vector_blocks(blocks, rows):
    blocks[...] = jnp.zeros_like(blocks)
    for p, row in enumerate(rows):
        half = row.shape[1] // 2
        stacked = jnp.concatenate([row[:, :half], row[:, half:], jnp.zeros((14, half), f32)], axis=0)
        blocks[p] = stacked.astype(bf16)


def emit_vectors(copies, pos, blocks, base, send, keep):
    for held, flip in ((send, 1), (keep, 0)):
        for zone in range(send.shape[0]):
            for q in range(4):
                owner = q * 2 + (pos[3] ^ flip)
                copies.add(blocks.at[owner], held.at[zone, q, pl.ds(base, 16), :])


def up_back(pos, grad_second, slope, normed, wd, vectors, last_sums, expo_out, send, keep, expos, hiddens, grad_up, up_sums, blocks, out_sems):
    step = pl.program_id(0)
    steps = pl.num_programs(0) - 1
    rows = normed.shape[0]
    width = normed.shape[1]

    @pl.when(step == 0)
    def _():
        up_sums[...] = jnp.zeros_like(up_sums)

    @pl.when(step < steps)
    def _():
        s = pl.ds(al(step * rows, 16), rows)
        low = grad_second[...].astype(bf16)
        chunk = 768
        for j in range(expos.shape[1] // chunk):
            c = slice(j * chunk, (j + 1) * chunk)
            grown = (nt(low, wd[c, :]) * slope[:, c].astype(f32)).astype(bf16)
            expos[s, c] = grown
            expo_out[:, c] = grown
            up_sums[0:1, c] += jnp.sum(grown.astype(f32), axis=0, keepdims=True)
        hiddens[s, :] = (normed[...] * vectors[3:4, :] + vectors[4:5, :]).astype(bf16)

    @pl.when(step == steps)
    def _():
        copies = Copies(out_sems)
        depth = grad_up.shape[0] // lax.axis_size("grp")
        chunk = 2 * COLS
        for j in range(grad_up.shape[1] // chunk):
            c = slice(j * chunk, (j + 1) * chunk)
            grad_up[:, c] = tn(hiddens[...], expos[:, c]).astype(bf16)
            emit(copies, pos, [("wide", grad_up, depth)], send, keep, (j,))
        rows_of = [last_sums[i : i + 1, :] for i in range(3)]
        rows_of += [up_sums[0:1, j * width : (j + 1) * width] for j in range(4)]
        vector_blocks(blocks, rows_of)
        emit_vectors(copies, pos, blocks, depth, send, keep)
        copies.wait()


def hidden_back(grad_second, expos, normed, inverse, mixed, wu, wo, vectors, grad_first, grad_mixed, sums, grad_out, lows):
    step = pl.program_id(0)
    steps = pl.num_programs(0) - 1
    rows = normed.shape[0]

    @pl.when(step == 0)
    def _():
        sums[...] = jnp.zeros_like(sums)

    @pl.when(step < steps)
    def _():
        s = pl.ds(al(step * rows, 16), rows)
        normal = normed[...]
        upstream = grad_second[...] + nt(expos[...], wu[...])
        result = norm_back(upstream, normal, inverse[:, 0:1], vectors[3:4, :])
        grad_first[...] = result
        low = result.astype(bf16)
        lows[s, :] = low
        grad_mixed[...] = nt(low, wo[...]).astype(bf16)
        sums[0:1, :] += jnp.sum(upstream * normal, axis=0, keepdims=True)
        sums[1:2, :] += jnp.sum(upstream, axis=0, keepdims=True)
        sums[2:3, :] += jnp.sum(low.astype(f32), axis=0, keepdims=True)

    @pl.when(step == steps)
    def _():
        grad_out[...] = tn(mixed[...], lows[...]).astype(bf16)


def heads_back(lengths, q, k, v, mixed, grad_mixed, logsum, held, deltas, sums, pair, first, count, width):
    slots = q.shape[0]
    span = q.shape[1]
    low = lax.broadcasted_iota(jnp.int32, (slots, 128), 1) < HD
    slot = lax.broadcasted_iota(jnp.int32, (slots, 1), 0)
    bias = jnp.where(slot < lengths[pair], 0.0, MASKED).astype(f32)
    product = mixed[...].astype(f32) * grad_mixed[...].astype(f32)
    select = (
        lax.broadcasted_iota(jnp.int32, (16, span), 1) // HD
        == lax.broadcasted_iota(jnp.int32, (16, span), 0)
    ).astype(bf16)
    high = product.astype(bf16)
    rest = (product - high.astype(f32)).astype(bf16)
    deltas[...] = nt(select, high) + nt(select, rest)
    here = pl.ds(al(pair * slots, 16), slots)
    scaling = HD ** (-0.5)

    def heads(h, carry):
        s = pl.ds(al(h * 128, 128), 128)
        q1, k1, v1, g1 = q[:, s], k[:, s], v[:, s], grad_mixed[:, s]
        probs, scores_back, qs, gs, ks = [], [], [], [], []
        for e in range(2):
            mask = low if e == 0 else ~low
            qm = jnp.where(mask, q1, 0).astype(bf16)
            gm = jnp.where(mask, g1, 0).astype(bf16)
            prob = jnp.exp(nt(k1, qm) + bias - logsum[0, pl.ds(first + h + 8 * e, 1), :])
            back = prob * (nt(v1, gm) - deltas[pl.ds(h * 2 + e, 1), :])
            probs.append(prob.astype(bf16))
            scores_back.append(back.astype(bf16))
            qs.append(qm)
            gs.append(gm)
            ks.append(jnp.where(mask, k1, 0).astype(bf16))
        grad_v = dot(jnp.concatenate(probs, 1), jnp.concatenate(gs, 0))
        grad_k = dot(jnp.concatenate(scores_back, 1), jnp.concatenate(qs, 0))
        grad_q = tn(jnp.concatenate(scores_back, 0), jnp.concatenate(ks, 0)) * scaling
        for m, value in enumerate((grad_q, grad_k, grad_v)):
            value = value.astype(bf16)
            held[here, pl.ds(al(m * span + h * 128, 128), 128)] = value
            if m != 1:
                sums[m : m + 1, pl.ds(al((first + h) * 128, 128), 128)] += jnp.sum(
                    value.astype(f32), axis=0, keepdims=True
                )
        return carry

    lax.fori_loop(0, count, heads, 0, unroll=True)


def attend_back(pos, lengths, x, q, k, v, mixed, grad_mixed, logsum, *rest, first, count):
    pair = pl.program_id(0)
    pairs = pl.num_programs(0) - 1
    if first == 0:
        grad_out, first_sums = rest[:2]
        grads, send, keep, sums, held, weight_grads, deltas, blocks, out_sems = rest[2:]
    else:
        old_sums = rest[0]
        grads, send, keep, held, weight_grads, deltas, sums, blocks, out_sems = rest[1:]

    @pl.when(pair == 0)
    def _():
        sums[...] = jnp.zeros_like(sums)

    @pl.when(pair < pairs)
    def _():
        heads_back(
            lengths, q, k, v, mixed, grad_mixed, logsum, held, deltas, sums, pair, first, count, x.shape[1]
        )
        slots = q.shape[0]
        grads[...] = held[pl.ds(al(pair * slots, 16), slots), :]

    @pl.when(pair == pairs)
    def _():
        span = q.shape[1]
        for m in range(3):
            c = slice(m * span, (m + 1) * span)
            weight_grads[:, c] = tn(x[...], held[:, c]).astype(bf16)
        copies = Copies(out_sems)
        depth = weight_grads.shape[0] // lax.axis_size("grp")
        if first == 0:
            parts = [("half", weight_grads, depth), ("0", grad_out, depth)]
            vectors = [first_sums[i : i + 1, :] for i in range(3)]
        else:
            parts = [("0", weight_grads, depth)]
            vectors = [sums[m : m + 1, :] + old_sums[m : m + 1, :] for m in (0, 2)]
        vector_blocks(blocks, vectors)
        emit(copies, pos, parts, send, keep)
        emit_vectors(copies, pos, blocks, block_rows(parts), send, keep)
        copies.wait()


def inputs_back(sofar, grads, weight, out, first):
    width = out.shape[1]
    total = sofar[...]
    span = grads.shape[1] // 3
    for m in range(3):
        c = slice(m * width + first, m * width + first + span)
        total = total + nt(grads[:, m * span : (m + 1) * span], weight[:, c])
    out[...] = total.astype(out.dtype)


def place_ffn(pos, shared, gd, gu, g2, s2, bd, bu):
    tall, half = gd.shape[0] // LOCAL, gu.shape[0] // 2
    n = shared.shape[0] // LOCAL
    for p in range(LOCAL):
        for j in range(2):
            at = p * n + j * tall
            gd[p * tall : (p + 1) * tall, j * COLS : (j + 1) * COLS] = shared[at : at + tall, :].astype(f32)
            at = p * n + 2 * tall + j * half
            first = (p // 2) * 2 * COLS + j * COLS
            rows = slice((p % 2) * half, (p % 2 + 1) * half)
            gu[rows, first : first + COLS] = shared[at : at + half, :].astype(f32)

    def vector(p):
        at = p * n + 2 * tall + 2 * half
        block = shared[at : at + 16, :].astype(f32)
        return jnp.concatenate([block[0:1, :], block[1:2, :]], axis=1)

    for p, out in enumerate((g2, s2, bd)):
        out[...] = own_part(pos, vector(p), out.shape[1])
    total = jnp.zeros(bu.shape, f32)
    for zone in range(4):
        total = jnp.where(pos[0] == zone, vector(3 + zone), total)
    bu[...] = total


def own_part(pos, row, size):
    total = row[:, :size]
    for zone in range(1, row.shape[1] // size):
        total = jnp.where(pos[0] == zone, row[:, zone * size : (zone + 1) * size], total)
    return total


def place_heads(pos, mine, sibling, gq, gk, gv, go, g1, s1, bo, bq, bv, cols_a, cols_b, small):
    depth = gq.shape[0]
    quarter, half = depth // 4, depth // 2
    n = mine.shape[0] // 4
    for sib, held in ((0, mine), (1, sibling)):
        for other in range(4):
            owner = pos[4] ^ (other * 2) ^ sib
            row4 = pl.ds(al((owner // 2) * quarter, 16), quarter)
            col2 = pl.ds(al((owner % 2) * COLS, 128), COLS)
            at = other * n
            cols_a[pl.ds(al((owner % 2) * half, 16), half), pl.ds(al((owner // 2) * COLS, 128), COLS)] = held[
                at : at + half, :
            ].astype(f32)
            at += half
            go[row4, col2] = held[at : at + quarter, :].astype(f32)
            at += quarter
            small[0, owner] = held[at : at + 16, :].astype(f32)[:8]
            at += 16
            cols_b[row4, col2] = held[at : at + quarter, :].astype(f32)
            at += quarter
            small[1, owner] = held[at : at + 16, :].astype(f32)[:8]
    for m, out in enumerate((gq, gk, gv)):
        span = cols_a.shape[1] // 3
        out[:, :span] = cols_a[:, m * span : (m + 1) * span]
        rest = cols_b.shape[1] // 3
        out[:, span:] = cols_b[:, m * rest : (m + 1) * rest]
    for out, which, p in ((g1, 0, 0), (s1, 0, 1), (bo, 0, 2), (bq, 1, 0), (bv, 1, 1)):
        block = small[which, p]
        row = jnp.concatenate([block[0:1, :], block[1:2, :]], axis=1)
        out[...] = own_part(pos, row, out.shape[1])


def shards(
    tokens,
    lengths,
    cotangent,
    query_weight,
    query_bias,
    key_weight,
    value_weight,
    value_bias,
    out_weight,
    out_bias,
    norm_gain,
    norm_shift,
    up_weight,
    up_bias,
    down_weight,
    down_bias,
    final_gain,
    final_shift,
):
    groups = lax.axis_size("grp")
    pairs, seqlen, width = tokens.shape
    rows = pairs * seqlen
    depth = width // groups
    wide = up_weight.shape[1]
    inputs = tokens.reshape(rows, width)
    upstream = cotangent.reshape(rows, width)
    pos = position()
    n1 = 3 * depth // 4
    n2 = depth + depth // 4
    n3 = depth

    def cut(kernel, sizes, args, specs):
        return pl.pallas_call(
            kernel,
            grid_spec=pltpu.PrefetchScalarGridSpec(
                num_scalar_prefetch=1,
                grid=(1,),
                in_specs=specs,
                out_specs=[pl.BlockSpec((n, COLS), lambda i, at: (0, 0)) for n in sizes],
            ),
            out_shape=[shape((n, COLS), bf16) for n in sizes],
            name=kernel.__name__,
        )(pos, *args)

    square = pl.BlockSpec((depth // 4, COLS), lambda i, at: (at[4] // 2, at[4] % 2))
    (first,) = cut(cut_first, (n1,), (query_weight, key_weight, value_weight), [square] * 3)
    z1 = [to_grp(first, step) for step in range(1, groups)]
    small = jnp.concatenate(
        after(
            [
                query_bias,
                value_bias,
                out_bias,
                norm_gain,
                norm_shift,
                down_bias,
                final_gain,
                final_shift,
                up_bias,
            ],
            first,
        )
    )
    count = small.shape[0] // COLS
    small = jnp.pad(small.reshape(count, COLS), ((0, 16 - count), (0, 0)))
    second, third = cut(
        cut_more,
        (n2 + 16, n3),
        (out_weight, up_weight, down_weight, small),
        [
            square,
            pl.BlockSpec((depth // 2, 2 * COLS), lambda i, at: (at[4] % 2, at[4] // 2)),
            pl.BlockSpec((down_weight.shape[0] // LOCAL, width), lambda i, at: (at[4], 0)),
            pl.BlockSpec((16, COLS), lambda i, at: (0, 0)),
        ],
    )

    def near(mine):
        return [mine, *(to_rep(mine, bit) for bit in (2, 4, 6))]

    def other_core(held):
        return [to_rep(part, 1) for part in held]

    def doubled(own):
        near_zone = to_grp(own, 1)
        pair = jnp.concatenate([own, near_zone], axis=0)
        return near_zone, to_grp(pair, 2)

    mine1 = jnp.concatenate(z1, axis=0)
    held1 = [mine1, to_rep(mine1, 2), to_rep(mine1, 4)]
    cut_at = (mine1.shape[0] // 2 + 47) // 48 * 48
    second = after(second, z1)
    parts = [second] + [to_grp(second, step) for step in range(1, groups)]
    held1 += [to_rep(held1[1][:cut_at], 4), to_rep(held1[2][cut_at:], 2)]
    held1 += other_core(held1)
    flat = jnp.stack([part[n2 : n2 + count].reshape(-1) for part in parts])
    by_zone = jnp.stack([flat[pos[0] ^ zone] for zone in range(groups)]).astype(f32)
    vectors = by_zone[:, : 8 * depth].reshape(groups, 8, depth).transpose(1, 0, 2).reshape(8, width)
    up_vector = by_zone[:, 8 * depth :].reshape(1, wide)
    mine2 = after(jnp.concatenate([part[:n2] for part in parts[1:]], axis=0), held1[:5])
    held2 = near(mine2)
    held2 += other_core(held2[:1])
    one, two = doubled(after(third, parts[1:]))

    row_block = 256
    blocks_of = rows // row_block
    mat = shape((rows, width), bf16)
    mat32 = shape((rows, width), f32)
    dense = 2 * rows * width * width
    by_pair = pl.BlockSpec((seqlen, width), lambda i: (i, 0))
    q, k, v, mixed, logsum, w_all = call(
        attend,
        (mat, mat, mat, mat, shape((pairs, 16, seqlen), f32), shape((width, 3 * width), bf16)),
        (pos, lengths, after(inputs, (mine2, one)), query_weight, key_weight, value_weight, vectors, *held1),
        [SMEM, SMEM, by_pair, ANY, ANY, ANY, VMEM] + [ANY] * 10,
        (by_pair,) * 4 + (pl.BlockSpec((1, 16, seqlen), lambda i: (i, 0, 0)), ANY),
        scratch=[
            pltpu.VMEM((width, 3 * width), bf16),
            pltpu.SemaphoreType.DMA((4 + 8 * (groups - 1) * 3,)),
        ],
        grid=(pairs,),
        flops=12 * dense,
        moved=12 * rows * width,
    )
    held2 += other_core(after(held2[1:4], (w_all, two)))
    held3 = near(jnp.concatenate([one, two], axis=0))
    held3 += other_core(held3[:1])
    by_row = pl.BlockSpec((row_block, width), lambda i: (i, 0))
    by_wide = pl.BlockSpec((row_block, wide), lambda i: (i, 0))
    by_lane = pl.BlockSpec((row_block, 128), lambda i: (i, 0))
    act, slope, normed, inverse, wu_all, wo_all = call(
        expand,
        (
            shape((rows, wide), bf16),
            shape((rows, wide), bf16),
            mat32,
            shape((rows, 128), f32),
            shape((width, wide), bf16),
            shape((width, width), bf16),
        ),
        (pos, after(inputs, held3[0]), mixed, up_weight, out_weight, vectors, up_vector, *held2),
        [SMEM, by_row, by_row, ANY, ANY, VMEM, VMEM] + [ANY] * 8,
        (by_wide, by_wide, by_row, by_lane, ANY, ANY),
        scratch=[
            pltpu.VMEM((width, wide), bf16),
            pltpu.VMEM((width, width), bf16),
            pltpu.SemaphoreType.DMA((4 + 8 * (groups - 1) * 3,)),
        ],
        grid=(blocks_of,),
        flops=8 * dense,
        moved=18 * rows * width,
    )
    held3 = after(held3, wo_all)
    held3 += other_core(held3[1:4])

    stay = lambda i: (jnp.minimum(i, blocks_of - 1), 0)
    by_row = pl.BlockSpec((row_block, width), stay)
    by_wide = pl.BlockSpec((row_block, wide), stay)
    by_lane = pl.BlockSpec((row_block, 128), stay)
    vec = shape((8, width), f32)
    vec_out = pl.BlockSpec((8, width), lambda i: (0, 0))

    def travelling(n):
        return (shape((groups, 4, n, COLS), bf16),) * 2

    output, grad_second, send, last_sums, wd_all = call(
        contract,
        (mat, mat32, shape((LOCAL, groups, n3, COLS), bf16), vec, shape((wide, width), bf16)),
        (pos, lengths, act, normed, upstream, down_weight, vectors, *held3),
        [SMEM, SMEM, ANY, by_row, by_row, ANY, VMEM] + [ANY] * 8,
        (by_row, by_row, ANY, vec_out, ANY),
        scratch=[
            pltpu.VMEM((wide, width), bf16),
            pltpu.VMEM((rows, wide), bf16),
            pltpu.VMEM((rows, width), bf16),
            pltpu.VMEM((wide, width), bf16),
            pltpu.SemaphoreType.DMA((4 + 8 * (groups - 1) * 2,)),
            pltpu.SemaphoreType.DMA((blocks_of,)),
            pltpu.SemaphoreType.DMA((groups * 4 * 2 * 2,)),
        ],
        grid=(blocks_of + 1,),
        flops=8 * dense,
        moved=16 * rows * width,
    )
    ring = lax.axis_size("rep")
    circles = [list(range(i, i + LOCAL)) for i in range(0, ring, LOCAL)] if ring > LOCAL else None
    down = lax.psum_scatter(
        send.reshape(LOCAL * groups * n3, COLS),
        "rep",
        scatter_dimension=0,
        tiled=True,
        axis_index_groups=circles,
    )

    n_up = depth + 16
    expos, send, keep = call(
        up_back,
        (shape((rows, wide), bf16), *travelling(n_up)),
        (pos, grad_second, slope, normed, wd_all, vectors, last_sums),
        [SMEM, by_row, by_wide, by_row, VMEM, VMEM, VMEM],
        (by_wide, ANY, ANY),
        scratch=[
            pltpu.VMEM((rows, wide), bf16),
            pltpu.VMEM((rows, width), bf16),
            pltpu.VMEM((width, wide), bf16),
            pltpu.VMEM((8, wide), f32),
            pltpu.VMEM((LOCAL, 16, COLS), bf16),
            pltpu.SemaphoreType.DMA((groups * 4 * 2 * 3,)),
        ],
        grid=(blocks_of + 1,),
        flops=8 * dense,
        moved=30 * rows * width,
    )
    up = Reduce(pos, send, keep)

    grad_first, grad_mixed, first_sums, grad_out = call(
        hidden_back,
        (mat32, mat, vec, shape((width, width), bf16)),
        (grad_second, expos, normed, inverse, mixed, wu_all, wo_all, vectors),
        [by_row, by_wide, by_row, by_lane, VMEM, VMEM, VMEM, VMEM],
        (by_row, by_row, vec_out, pl.BlockSpec((width, width), lambda i: (0, 0))),
        scratch=[pltpu.VMEM((rows, width), bf16)],
        grid=(blocks_of + 1,),
        flops=6 * dense,
        moved=30 * rows * width,
    )
    done = up.one(grad_mixed)

    def heads_call(first, count, n, extra, extra_specs, done, sums_out):
        span = count * 128
        part = lambda i: (jnp.minimum(i, pairs - 1), first * 128 // span)
        by_pair = pl.BlockSpec((seqlen, span), part)
        outs = (shape((rows, 3 * span), bf16), *travelling(n)) + ((vec,) if sums_out else ())
        out_specs = (
            pl.BlockSpec((seqlen, 3 * span), lambda i: (jnp.minimum(i, pairs - 1), 0)),
            ANY,
            ANY,
        ) + ((vec_out,) if sums_out else ())
        scratch = [
            pltpu.VMEM((rows, 3 * span), bf16),
            pltpu.VMEM((width, 3 * span), bf16),
            pltpu.VMEM((16, seqlen), f32),
        ]
        scratch += [] if sums_out else [pltpu.VMEM((8, width), f32)]
        scratch += [
            pltpu.VMEM((LOCAL, 16, COLS), bf16),
            pltpu.SemaphoreType.DMA((groups * 4 * 2 * 3,)),
        ]
        return call(
            attend_back,
            outs,
            (pos, lengths, after(inputs, done), q, k, v, mixed, grad_mixed, logsum, *extra),
            [SMEM, SMEM, VMEM]
            + [by_pair] * 5
            + [pl.BlockSpec((1, 16, seqlen), lambda i: (jnp.minimum(i, pairs - 1), 0, 0))]
            + extra_specs,
            out_specs,
            scratch=scratch,
            grid=(pairs + 1,),
            flops=4 * dense * count,
            moved=4 * rows * width * count,
            first=first,
            count=count,
        )

    grads_a, send, keep, sums = heads_call(
        0, 4, depth // 2 + depth // 4 + 16, (grad_out, first_sums), [VMEM, VMEM], done, True
    )
    part_a = Reduce(pos, send, keep)
    by_row = pl.BlockSpec((row_block, width), lambda i: (i, 0))

    def inputs_call(sofar, grads, first, last, dtype):
        return call(
            inputs_back,
            shape((rows, width), dtype),
            (sofar, grads, w_all),
            [by_row, pl.BlockSpec((row_block, grads.shape[1]), lambda i: (i, 0)), VMEM],
            by_row,
            grid=(blocks_of,),
            flops=dense * grads.shape[1] // width,
            moved=16 * rows * width,
            first=first,
        )

    done = up.two(grads_a)
    sofar = inputs_call(after(grad_first, done), grads_a, 0, False, f32)
    done = part_a.one(sofar)
    grads_b, send, keep = heads_call(4, 2, depth // 4 + 16, (sums,), [VMEM], done, False)
    part_b = Reduce(pos, send, keep)
    total = up.zones(down.reshape(groups, n3, COLS), grads_b)
    total = lax.psum_scatter(total.reshape(-1, COLS), "grp", scatter_dimension=0, tiled=True)
    done = (part_a.two(grads_b), part_b.direct(grads_b))
    grad_inputs = inputs_call(after(sofar, done), grads_b, grads_a.shape[1] // 3, True, bf16)
    done = part_a.three_with(part_b, grad_inputs)
    shared = lax.all_gather(
        over_blocks(after(total, done)), "rep", axis=0, tiled=True, axis_index_groups=circles
    )
    part_a.four()
    part_a.around()
    part_a.five()
    vector = shape((1, depth), f32)
    gd, gu, g2, s2, bd, bu = call(
        place_ffn,
        (shape((wide // groups, width), f32), shape((depth, wide), f32), vector, vector, vector)
        + (shape((1, wide // groups), f32),),
        (pos, shared),
        [SMEM, VMEM],
        (VMEM,) * 6,
        moved=24 * depth * width,
    )
    square = shape((depth, width), f32)
    gq, gk, gv, go, g1, s1, bo, bq, bv = call(
        place_heads,
        (square,) * 4 + (vector,) * 5,
        (pos, *part_a.both),
        [SMEM] + [VMEM] * 2,
        (VMEM,) * 9,
        scratch=[
            pltpu.VMEM((depth, 2 * width), f32),
            pltpu.VMEM((depth, width), f32),
            pltpu.VMEM((2, LOCAL, 8, COLS), f32),
        ],
        moved=24 * depth * width,
    )
    bq, bv, bo, g1, s1, bu, bd, g2, s2 = (
        row.reshape(-1) for row in (bq, bv, bo, g1, s1, bu, bd, g2, s2)
    )
    return (
        output.reshape(pairs, seqlen, width),
        grad_inputs.reshape(pairs, seqlen, width),
        gq,
        bq,
        gk,
        gv,
        bv,
        go,
        bo,
        g1,
        s1,
        gu,
        bu,
        gd,
        bd,
        g2,
        s2,
    )


def solution(mesh):
    pairs = P(("grp", "rep"), None, None)
    matrix = P("grp", None)
    vector = P("grp")
    placed = (pairs, P(("grp", "rep")), pairs, matrix, vector, matrix, matrix, vector, matrix, vector)
    placed += (vector, vector, matrix, vector, matrix, vector, vector, vector)
    results = (pairs, pairs, matrix, vector, matrix, matrix, vector, matrix, vector, vector, vector)
    results += (matrix, vector, matrix, vector, vector, vector)
    return jax.shard_map(shards, mesh=mesh, in_specs=placed, out_specs=results, check_vma=False)
```

profile of v0, /device:TPU:0, one launch (start us, length us, event | category | flops | bytes accessed | tf_op | source)
XLA Modules:
  0.0 338.7 jit_solution(12813351622078402486)
XLA Ops:
  10.0 5.0 %collective-permute-start.2 = (bf16[144,384]{1,0:T(8,128)(2,1)}, bf16[144,384]{1,0:T(8,128)(2,1)S(1)}, u32[]{:S(2)}, u32[]{:S(2)}) collective-permute-start(bf16[144,384]{1,0:T(8,128)(2,1)} %cut_first.1), channel_id=1, source_target_pairs={{0,24},{8,16},{16,8},{24,0},{1,25},{9,17},{17,9},{25,1},{2,26},{10... | collective-permute-start | bytes 331784 | tf_op jit(solution)/shard_map/ppermute | solution.py:76
  15.6 6.1 %concatenate.18 = bf16[2304]{0:T(1024)(128)(2,1)S(1)} concatenate(bf16[192]{0:T(256)(128)(2,1)} %param.22, bf16[192]{0:T(256)(128)(2,1)} %param.25, bf16[192]{0:T(256)(128)(2,1)} %param.27, bf16[192]{0:T(256)(128)(2,1)} %param.28, bf16[192]{0:T(256)(128)(2,1)} %param.29, bf16[192]{0:T(256)(128)(2,1)} %param.33, bf16[192]{0:T(256)(128)(2,1)} %param.34, bf16[192]{0:T(256)(128)(2,1)} %param.35, ...), dimensions={0} | concatenate | bytes 9216 | tf_op jit(solution)/shard_map/concatenate | solution.py:858
  24.8 3.9 %collective-permute-start.5 = (bf16[256,384]{1,0:T(8,128)(2,1)}, bf16[256,384]{1,0:T(8,128)(2,1)S(1)}, u32[]{:S(2)}, u32[]{:S(2)}) collective-permute-start(bf16[256,384]{1,0:T(8,128)(2,1)} %get-tuple-element.147), channel_id=1, source_target_pairs={{0,24},{8,16},{16,8},{24,0},{1,25},{9,17},{17,9},{25,1},{2,26},{10... | collective-permute-start | bytes 589832 | tf_op jit(solution)/shard_map/ppermute | solution.py:76
  36.5 8.2 %collective-permute-done.4 = bf16[256,384]{1,0:T(8,128)(2,1)S(1)} collective-permute-done((bf16[256,384]{1,0:T(8,128)(2,1)}, bf16[256,384]{1,0:T(8,128)(2,1)S(1)}, u32[]{:S(2)}, u32[]{:S(2)}) %collective-permute-start.4) | collective-permute-done | bytes 196640 | tf_op jit(solution)/shard_map/ppermute | solution.py:76
  54.7 5.9 %collective-permute-start.7 = (bf16[384,384]{1,0:T(8,128)(2,1)}, bf16[384,384]{1,0:T(8,128)(2,1)}, u32[]{:S(2)}, u32[]{:S(2)}) collective-permute-start(bf16[384,384]{1,0:T(8,128)(2,1)} %pad_maximum_fusion.2), channel_id=1, source_target_pairs={{0,16},{8,24},{16,0},{24,8},{1,17},{9,25},{17,1},{25,9},{2,18},{10... | collective-permute-start | bytes 884744 | tf_op jit(solution)/shard_map/ppermute | solution.py:76
  64.5 18.4 %attend.1 = (bf16[1024,768]{1,0:T(8,128)(2,1)}, bf16[1024,768]{1,0:T(8,128)(2,1)}, bf16[1024,768]{1,0:T(8,128)(2,1)}, bf16[1024,768]{1,0:T(8,128)(2,1)}, f32[2,1...) custom-call(s32[5]{0:T(128)} %stack.29.pos, s32[2]{0:T(128)} %lengths.7, bf16[1024,768]{1,0:T(8,128)(2,1)} %bitcast.51, ...), custom_call_target="tpu_custom_call" | custom-call | flops 289910292480 | bytes 188743680 | tf_op jit(solution)/shard_map/attend/pallas_call | solution.py:49
  82.9 5.8 %collective-permute-done.18.rest_2_ = bf16[720,384]{1,0:T(8,128)(2,1)} collective-permute-done((bf16[720,384]{1,0:T(8,128)(2,1)}, bf16[720,384]{1,0:T(8,128)(2,1)}, u32[]{:S(2)}, u32[]{:S(2)}) %collective-permute-start.18) | collective-permute-done | bytes 552992 | tf_op jit(solution)/shard_map/ppermute | solution.py:71
  98.0 19.6 %expand.1 = (bf16[1024,3072]{1,0:T(8,128)(2,1)}, bf16[1024,3072]{1,0:T(8,128)(2,1)}, f32[1024,768]{1,0:T(8,128)}, f32[1024,128]{1,0:T(8,128)}, bf16[768,3072]{1,0:T(8,128)(2,1)}, /*index=5*/bf16[768,768]{1,0:T(8,128)(2,1)}) custom-call(s32[5]{0:T(128)} %stack.29.pos, bf16[1024,768]{1,0:T(8,128)(2,1)} %bitcast.52, ...), custom_call_target="tpu_custom_call" | custom-call | flops 193273528320 | bytes 283115520 | tf_op jit(solution)/shard_map/expand/pallas_call | solution.py:49
  121.7 22.2 %contract.1 = (bf16[1024,768]{1,0:T(8,128)(2,1)}, f32[1024,768]{1,0:T(8,128)}, bf16[8,4,192,384]{3,2,1,0:T(8,128)(2,1)}, f32[8,768]{1,0:T(8,128)}, bf16[3072,768]{1,0:T(8,128)(2,1)}) custom-call(s32[5]{0:T(128)} %stack.29.pos, s32[2]{0:T(128)} %lengths.7, bf16[1024,3072]{1,0:T(8,128)(2,1)} %get-tuple-element.157.act, f32[1024,768]{1,0:T(8,128)} %get-tuple-element.158.normed, ...), custom_call_target="tpu_custom_call" | custom-call | flops 193273528320 | bytes 251658240 | tf_op jit(solution)/shard_map/contract/pallas_call | solution.py:49
  144.0 21.3 %up_back.1 = (bf16[1024,3072]{1,0:T(8,128)(2,1)}, bf16[4,4,208,384]{3,2,1,0:T(8,128)(2,1)}, bf16[4,4,208,384]{3,2,1,0:T(8,128)(2,1)}) custom-call(s32[5]{0:T(128)} %stack.29.pos, f32[1024,768]{1,0:T(8,128)} %get-tuple-element.166.grad_second, bf16[1024,3072]{1,0:T(8,128)(2,1)} %get-tuple-element.167.slope, f32[1024,768]{1,0:T(8,128)} %get-tuple-element.158.normed, ...), custom_call_target="tpu_custom_call" | custom-call | flops 193273528320 | bytes 471859200 | tf_op jit(solution)/shard_map/up_back/pallas_call | solution.py:49
  165.6 18.2 %hidden_back.1 = (f32[1024,768]{1,0:T(8,128)}, bf16[1024,768]{1,0:T(8,128)(2,1)}, f32[8,768]{1,0:T(8,128)}, bf16[768,768]{1,0:T(8,128)(2,1)}) custom-call(f32[1024,768]{1,0:T(8,128)} %get-tuple-element.166.grad_second, bf16[1024,3072]{1,0:T(8,128)(2,1)} %get-tuple-element.170.expos, f32[1024,768]{1,0:T(8,128)} %get-tuple-element.158.normed, ...), custom_call_target="tpu_custom_call" | custom-call | flops 144955146240 | bytes 471859200 | tf_op jit(solution)/shard_map/hidden_back/pallas_call | solution.py:49
  183.7 4.4 %add_first.2 = (bf16[2,2,208,384]{3,2,1,0:T(8,128)(2,1)}, bf16[2,2,208,384]{3,2,1,0:T(8,128)(2,1)}, bf16[2,2,208,384]{3,2,1,0:T(8,128)(2,1)}, bf16[2,2,208,384]{3,2,1,0:T(8,128)(2,1)}) custom-call(s32[5]{0:T(128)} %stack.29.pos, bf16[4,4,208,384]{3,2,1,0:T(8,128)(2,1)} %get-tuple-element.174.keep, bf16[4,4,208,384]{3,2,1,0:T(8,128)(2,1)} %collective-permute-done.31.got), custom_call_target="tpu_custom_call" | custom-call | bytes 153354240 | tf_op jit(solution)/shard_map/add_first/pallas_call | solution.py:49
  190.3 22.6 %attend_back.2 = (bf16[1024,1536]{1,0:T(8,128)(2,1)}, bf16[4,4,160,384]{3,2,1,0:T(8,128)(2,1)}, bf16[4,4,160,384]{3,2,1,0:T(8,128)(2,1)}, f32[8,768]{1,0:T(8,128)}) custom-call(s32[5]{0:T(128)} %stack.29.pos, s32[2]{0:T(128)} %lengths.7, bf16[1024,768]{1,0:T(8,128)(2,1)} %bitcast.53, bf16[1024,768]{1,0:T(8,128)(2,1)} %get-tuple-element.182.q, ...), custom_call_target="tpu_custom_call" | custom-call | flops 386547056640 | bytes 251658240 | tf_op jit(solution)/shard_map/attend_back/pallas_call | solution.py:49
  215.9 7.6 %inputs_back.2.sofar = f32[1024,768]{1,0:T(8,128)} custom-call(f32[1024,768]{1,0:T(8,128)} %get-tuple-element.193.sofar, bf16[1024,1536]{1,0:T(8,128)(2,1)} %get-tuple-element.188.grads, bf16[768,2304]{1,0:T(8,128)(2,1)} %get-tuple-element.153.weight), custom_call_target="tpu_custom_call" | custom-call | flops 48318382080 | bytes 251658240 | tf_op jit(solution)/shard_map/inputs_back/pallas_call | solution.py:49
  224.9 3.7 %add_first.3 = (bf16[2,2,160,384]{3,2,1,0:T(8,128)(2,1)}, bf16[2,2,160,384]{3,2,1,0:T(8,128)(2,1)}, bf16[2,2,160,384]{3,2,1,0:T(8,128)(2,1)}, bf16[2,2,160,384]{3,2,1,0:T(8,128)(2,1)}) custom-call(s32[5]{0:T(128)} %stack.29.pos, bf16[4,4,160,384]{3,2,1,0:T(8,128)(2,1)} %get-tuple-element.194.keep, bf16[4,4,160,384]{3,2,1,0:T(8,128)(2,1)} %copy-done.1), custom_call_target="tpu_custom_call" | custom-call | bytes 117964800 | tf_op jit(solution)/shard_map/add_first/pallas_call | solution.py:49
  228.6 13.4 %attend_back.3 = (bf16[1024,768]{1,0:T(8,128)(2,1)}, bf16[4,4,64,384]{3,2,1,0:T(8,128)(2,1)}, bf16[4,4,64,384]{3,2,1,0:T(8,128)(2,1)}) custom-call(s32[5]{0:T(128)} %stack.29.pos, s32[2]{0:T(128)} %lengths.7, bf16[1024,768]{1,0:T(8,128)(2,1)} %bitcast.54, bf16[1024,768]{1,0:T(8,128)(2,1)} %get-tuple-element.182.q, bf16[1024,768]{1,0:T(8,128)(2,1)} %get-tuple-element.183.k, ...), custom_call_target="tpu_custom_call" | custom-call | flops 193273528320 | bytes 125829120 | tf_op jit(solution)/shard_map/attend_back/pallas_call | solution.py:49
  246.6 6.3 %collective-permute-done.50.ra = bf16[2,208,384]{2,1,0:T(8,128)(2,1)S(1)} collective-permute-done((bf16[2,208,384]{2,1,0:T(8,128)(2,1)S(1)}, bf16[2,208,384]{2,1,0:T(8,128)(2,1)S(1)}, u32[]{:S(2)}, u32[]{:S(2)}) %collective-permute-start.50) | collective-permute-done | bytes 319520 | tf_op jit(solution)/shard_map/ppermute | solution.py:71
  257.6 5.9 %collective-permute-done.35.ra = bf16[2,2,160,384]{3,2,1,0:T(8,128)(2,1)S(1)} collective-permute-done((bf16[2,2,160,384]{3,2,1,0:T(8,128)(2,1)S(1)}, bf16[2,2,160,384]{3,2,1,0:T(8,128)(2,1)S(1)}, u32[]{:S(2)}, u32[]{:S(2)}) %collective-permute-start.35) | collective-permute-done | bytes 491552 | tf_op jit(solution)/shard_map/ppermute | solution.py:71
  275.8 6.5 %inputs_back.3 = bf16[1024,768]{1,0:T(8,128)(2,1)} custom-call(f32[1024,768]{1,0:T(8,128)} %inputs_back.2.sofar, bf16[1024,768]{1,0:T(8,128)(2,1)} %get-tuple-element.202.grads, bf16[768,2304]{1,0:T(8,128)(2,1)} %get-tuple-element.153.weight), custom_call_target="tpu_custom_call" | custom-call | flops 24159191040 | bytes 251658240 | tf_op jit(solution)/shard_map/inputs_back/pallas_call | solution.py:49
  291.4 3.1 collective-permute-done.43.refs_1_
  294.6 7.7 %collective-permute-done.44.refs_2_ = bf16[224,384]{1,0:T(8,128)(2,1)S(1)} collective-permute-done((bf16[224,384]{1,0:T(8,128)(2,1)}, bf16[224,384]{1,0:T(8,128)(2,1)S(1)}, u32[]{:S(2)}, u32[]{:S(2)}) %collective-permute-start.44) | collective-permute-done | bytes 172064 | tf_op jit(solution)/shard_map/ppermute | solution.py:76
  309.0 7.3 %collective-permute-done.48 = bf16[224,384]{1,0:T(8,128)(2,1)S(1)} collective-permute-done((bf16[224,384]{1,0:T(8,128)(2,1)}, bf16[224,384]{1,0:T(8,128)(2,1)S(1)}, u32[]{:S(2)}, u32[]{:S(2)}) %collective-permute-start.48) | collective-permute-done | bytes 172064 | tf_op jit(solution)/shard_map/ppermute | solution.py:71
  323.4 3.0 place_heads.1
  326.4 4.3 %place_ffn.1 = (f32[768,768]{1,0:T(8,128)}, f32[192,3072]{1,0:T(8,128)}, f32[1,192]{1,0:T(1,128)}, f32[1,192]{1,0:T(1,128)}, f32[1,192]{1,0:T(1,128)}, /*index=5*/f32[1,768]{1,0:T(1,128)}) custom-call(s32[5]{0:T(128)} %stack.29.pos, bf16[3200,384]{1,0:T(8,128)(2,1)} %all-gather.2.cloned.1.call-done.shared), custom_call_target="tpu_custom_call" | custom-call | bytes 70778880 | tf_op jit(solution)/shard_map/place_ffn/pallas_call | solution.py:49
  (237 shorter events, 93.7 us)
Async XLA Ops:
  7.2 247.0 %reduce-scatter.3.cloned.1.call-start = ((), (), s32[]{:S(2)}) async-start(), calls=%async_computation.2 | async-start | bytes 5308416 | tf_op jit(solution)/shard_map/reduce_scatter | solution.py:997
  28.7 16.0 %collective-permute-start.4 = (bf16[256,384]{1,0:T(8,128)(2,1)}, bf16[256,384]{1,0:T(8,128)(2,1)S(1)}, u32[]{:S(2)}, u32[]{:S(2)}) collective-permute-start(bf16[256,384]{1,0:T(8,128)(2,1)} %get-tuple-element.147), channel_id=1, source_target_pairs={{0,16},{8,24},{16,0},{24,8},{1,17},{9,25},{17,1},{25,9},{2,18},{10... | collective-permute-start | bytes 589832 | tf_op jit(solution)/shard_map/ppermute | solution.py:76
  28.7 16.0 %collective-permute-start.3 = (bf16[256,384]{1,0:T(8,128)(2,1)}, bf16[256,384]{1,0:T(8,128)(2,1)S(1)}, u32[]{:S(2)}, u32[]{:S(2)}) collective-permute-start(bf16[256,384]{1,0:T(8,128)(2,1)} %get-tuple-element.147), channel_id=1, source_target_pairs={{0,8},{8,0},{16,24},{24,16},{1,9},{9,1},{17,25},{25,17},{2,10},{10... | collective-permute-start | bytes 589832 | tf_op jit(solution)/shard_map/ppermute | solution.py:76
  29.5 25.3 %collective-permute-start.12 = (bf16[432,384]{1,0:T(8,128)(2,1)S(1)}, bf16[432,384]{1,0:T(8,128)(2,1)S(1)}, u32[]{:S(2)}, u32[]{:S(2)}) collective-permute-start(bf16[432,384]{1,0:T(8,128)(2,1)S(1)} %constant_dynamic-update-slice_fusion.2.rest_0_), channel_id=1, source_target_pairs={{0,1},{1,0},{2,3},{3,2},{4,5},{5,4},{6,7},{7,6},{8,9},{9,8},{10,11... | collective-permute-start | bytes 995336 | tf_op jit(solution)/shard_map/ppermute | solution.py:71
  29.5 15.5 %collective-permute-start.9 = (bf16[432,384]{1,0:T(8,128)(2,1)S(1)}, bf16[432,384]{1,0:T(8,128)(2,1)S(1)}, u32[]{:S(2)}, u32[]{:S(2)}) collective-permute-start(bf16[432,384]{1,0:T(8,128)(2,1)S(1)} %constant_dynamic-update-slice_fusion.2.rest_0_), channel_id=1, source_target_pairs={{0,4},{1,5},{2,6},{3,7},{4,0},{5,1},{6,2},{7,3},{8,12},{9,13},{10,... | collective-permute-start | bytes 995336 | tf_op jit(solution)/shard_map/ppermute | solution.py:71
  54.7 28.1 %collective-permute-start.7 = (bf16[384,384]{1,0:T(8,128)(2,1)}, bf16[384,384]{1,0:T(8,128)(2,1)}, u32[]{:S(2)}, u32[]{:S(2)}) collective-permute-start(bf16[384,384]{1,0:T(8,128)(2,1)} %pad_maximum_fusion.2), channel_id=1, source_target_pairs={{0,16},{8,24},{16,0},{24,8},{1,17},{9,25},{17,1},{25,9},{2,18},{10... | collective-permute-start | bytes 884744 | tf_op jit(solution)/shard_map/ppermute | solution.py:76
  60.6 33.1 %collective-permute-start.20 = (bf16[720,384]{1,0:T(8,128)(2,1)}, bf16[720,384]{1,0:T(8,128)(2,1)}, u32[]{:S(2)}, u32[]{:S(2)}) collective-permute-start(bf16[720,384]{1,0:T(8,128)(2,1)} %pad_maximum_fusion.1.rest_0_), channel_id=1, source_target_pairs={{0,1},{1,0},{2,3},{3,2},{4,5},{5,4},{6,7},{7,6},{8,9},{9,8},{10,11... | collective-permute-start | bytes 1658888 | tf_op jit(solution)/shard_map/ppermute | solution.py:71
  60.8 22.0 %collective-permute-start.19 = (bf16[720,384]{1,0:T(8,128)(2,1)}, bf16[720,384]{1,0:T(8,128)(2,1)}, u32[]{:S(2)}, u32[]{:S(2)}) collective-permute-start(bf16[720,384]{1,0:T(8,128)(2,1)} %pad_maximum_fusion.1.rest_0_), channel_id=1, source_target_pairs={{0,6},{1,7},{2,4},{3,5},{4,2},{5,3},{6,0},{7,1},{8,14},{9,15},{10,... | collective-permute-start | bytes 1658888 | tf_op jit(solution)/shard_map/ppermute | solution.py:71
  63.3 25.3 %collective-permute-start.18 = (bf16[720,384]{1,0:T(8,128)(2,1)}, bf16[720,384]{1,0:T(8,128)(2,1)}, u32[]{:S(2)}, u32[]{:S(2)}) collective-permute-start(bf16[720,384]{1,0:T(8,128)(2,1)} %pad_maximum_fusion.1.rest_0_), channel_id=1, source_target_pairs={{0,4},{1,5},{2,6},{3,7},{4,0},{5,1},{6,2},{7,3},{8,12},{9,13},{10,... | collective-permute-start | bytes 1658888 | tf_op jit(solution)/shard_map/ppermute | solution.py:71
  63.8 24.9 %collective-permute-start.17 = (bf16[720,384]{1,0:T(8,128)(2,1)}, bf16[720,384]{1,0:T(8,128)(2,1)}, u32[]{:S(2)}, u32[]{:S(2)}) collective-permute-start(bf16[720,384]{1,0:T(8,128)(2,1)} %pad_maximum_fusion.1.rest_0_), channel_id=1, source_target_pairs={{0,2},{1,3},{2,0},{3,1},{4,6},{5,7},{6,4},{7,5},{8,10},{9,11},{10,... | collective-permute-start | bytes 1658888 | tf_op jit(solution)/shard_map/ppermute | solution.py:71
  93.2 24.4 %collective-permute-start.27 = (bf16[576,384]{1,0:T(8,128)(2,1)}, bf16[576,384]{1,0:T(8,128)(2,1)}, u32[]{:S(2)}, u32[]{:S(2)}) collective-permute-start(bf16[576,384]{1,0:T(8,128)(2,1)} %constant_dynamic-update-slice_fusion.rest_0_), channel_id=1, source_target_pairs={{0,1},{1,0},{2,3},{3,2},{4,5},{5,4},{6,7},{7,6},{8,9},{9,8},{10,11... | collective-permute-start | bytes 1327112 | tf_op jit(solution)/shard_map/ppermute | solution.py:71
  93.7 23.9 %collective-permute-start.26 = (bf16[576,384]{1,0:T(8,128)(2,1)}, bf16[576,384]{1,0:T(8,128)(2,1)}, u32[]{:S(2)}, u32[]{:S(2)}) collective-permute-start(bf16[576,384]{1,0:T(8,128)(2,1)} %constant_dynamic-update-slice_fusion.rest_0_), channel_id=1, source_target_pairs={{0,6},{1,7},{2,4},{3,5},{4,2},{5,3},{6,0},{7,1},{8,14},{9,15},{10,... | collective-permute-start | bytes 1327112 | tf_op jit(solution)/shard_map/ppermute | solution.py:71
  95.4 22.2 %collective-permute-start.25 = (bf16[576,384]{1,0:T(8,128)(2,1)}, bf16[576,384]{1,0:T(8,128)(2,1)}, u32[]{:S(2)}, u32[]{:S(2)}) collective-permute-start(bf16[576,384]{1,0:T(8,128)(2,1)} %constant_dynamic-update-slice_fusion.rest_0_), channel_id=1, source_target_pairs={{0,4},{1,5},{2,6},{3,7},{4,0},{5,1},{6,2},{7,3},{8,12},{9,13},{10,... | collective-permute-start | bytes 1327112 | tf_op jit(solution)/shard_map/ppermute | solution.py:71
  96.7 20.9 %collective-permute-start.24 = (bf16[576,384]{1,0:T(8,128)(2,1)}, bf16[576,384]{1,0:T(8,128)(2,1)}, u32[]{:S(2)}, u32[]{:S(2)}) collective-permute-start(bf16[576,384]{1,0:T(8,128)(2,1)} %constant_dynamic-update-slice_fusion.rest_0_), channel_id=1, source_target_pairs={{0,2},{1,3},{2,0},{3,1},{4,6},{5,7},{6,4},{7,5},{8,10},{9,11},{10,... | collective-permute-start | bytes 1327112 | tf_op jit(solution)/shard_map/ppermute | solution.py:71
  144.0 143.0 %reduce-scatter.5.cloned.1.call-start = ((), (), s32[]{:S(2)}) async-start(), calls=%async_computation.3 | async-start | bytes 1536000 | tf_op jit(solution)/shard_map/reduce_scatter | solution.py:1101
  165.3 18.4 %collective-permute-start.31 = (bf16[4,4,208,384]{3,2,1,0:T(8,128)(2,1)}, bf16[4,4,208,384]{3,2,1,0:T(8,128)(2,1)}, u32[]{:S(2)}, u32[]{:S(2)}) collective-permute-start(bf16[4,4,208,384]{3,2,1,0:T(8,128)(2,1)} %get-tuple-element.175), channel_id=1, source_target_pairs={{0,1},{1,0},{2,3},{3,2},{4,5},{5,4},{6,7},{7,6},{8,9},{9,8},{10,11... | collective-permute-start | bytes 7667720 | tf_op jit(solution)/shard_map/ppermute | solution.py:71
  188.1 24.9 %collective-permute-start.32 = (bf16[2,2,208,384]{3,2,1,0:T(8,128)(2,1)}, bf16[2,2,208,384]{3,2,1,0:T(8,128)(2,1)}, u32[]{:S(2)}, u32[]{:S(2)}) collective-permute-start(bf16[2,2,208,384]{3,2,1,0:T(8,128)(2,1)} %get-tuple-element.179), channel_id=1, source_target_pairs={{0,2},{1,3},{2,0},{3,1},{4,6},{5,7},{6,4},{7,5},{8,10},{9,11},{10,... | collective-permute-start | bytes 1916936 | tf_op jit(solution)/shard_map/ppermute | solution.py:71
  189.5 23.5 %collective-permute-start.33 = (bf16[2,2,208,384]{3,2,1,0:T(8,128)(2,1)}, bf16[2,2,208,384]{3,2,1,0:T(8,128)(2,1)}, u32[]{:S(2)}, u32[]{:S(2)}) collective-permute-start(bf16[2,2,208,384]{3,2,1,0:T(8,128)(2,1)} %get-tuple-element.180), channel_id=1, source_target_pairs={{0,4},{1,5},{2,6},{3,7},{4,0},{5,1},{6,2},{7,3},{8,12},{9,13},{10,... | collective-permute-start | bytes 1916936 | tf_op jit(solution)/shard_map/ppermute | solution.py:71
  242.0 27.1 %collective-permute-start.37 = (bf16[4,4,64,384]{3,2,1,0:T(8,128)(2,1)}, bf16[4,4,64,384]{3,2,1,0:T(8,128)(2,1)S(1)}, u32[]{:S(2)}, u32[]{:S(2)}) collective-permute-start(bf16[4,4,64,384]{3,2,1,0:T(8,128)(2,1)} %get-tuple-element.208), channel_id=1, source_target_pairs={{0,1},{1,0},{2,3},{3,2},{4,5},{5,4},{6,7},{7,6},{8,9},{9,8},{10,11... | collective-permute-start | bytes 2359304 | tf_op jit(solution)/shard_map/ppermute | solution.py:71
  244.4 19.1 %collective-permute-start.35 = (bf16[2,2,160,384]{3,2,1,0:T(8,128)(2,1)S(1)}, bf16[2,2,160,384]{3,2,1,0:T(8,128)(2,1)S(1)}, u32[]{:S(2)}, u32[]{:S(2)}) collective-permute-start(bf16[2,2,160,384]{3,2,1,0:T(8,128)(2,1)S(1)} %copy-done.33), channel_id=1, source_target_pairs={{0,2},{1,3},{2,0},{3,1},{4,6},{5,7},{6,4},{7,5},{8,10},{9,11},{10,... | collective-permute-start | bytes 1474568 | tf_op jit(solution)/shard_map/ppermute | solution.py:71
  245.8 17.8 %collective-permute-start.36 = (bf16[2,2,160,384]{3,2,1,0:T(8,128)(2,1)S(1)}, bf16[2,2,160,384]{3,2,1,0:T(8,128)(2,1)S(1)}, u32[]{:S(2)}, u32[]{:S(2)}) collective-permute-start(bf16[2,2,160,384]{3,2,1,0:T(8,128)(2,1)S(1)} %copy-done.32), channel_id=1, source_target_pairs={{0,4},{1,5},{2,6},{3,7},{4,0},{5,1},{6,2},{7,3},{8,12},{9,13},{10,... | collective-permute-start | bytes 1474568 | tf_op jit(solution)/shard_map/ppermute | solution.py:71
  257.5 68.9 %all-gather.2.cloned.1.call-start = ((), (), s32[]{:S(2)}) async-start(), calls=%async_computation.4 | async-start | bytes 2764800 | tf_op jit(solution)/shard_map/all_gather | solution.py:1105
  267.0 15.2 %collective-permute-start.38 = (bf16[2,160,384]{2,1,0:T(8,128)(2,1)}, bf16[2,160,384]{2,1,0:T(8,128)(2,1)S(1)}, u32[]{:S(2)}, u32[]{:S(2)}) collective-permute-start(bf16[2,160,384]{2,1,0:T(8,128)(2,1)} %get-tuple-element.212), channel_id=1, source_target_pairs={{0,4},{1,5},{2,6},{3,7},{4,0},{5,1},{6,2},{7,3},{8,12},{9,13},{10,... | collective-permute-start | bytes 737288 | tf_op jit(solution)/shard_map/ppermute | solution.py:71
  287.0 15.2 %collective-permute-start.44 = (bf16[224,384]{1,0:T(8,128)(2,1)}, bf16[224,384]{1,0:T(8,128)(2,1)S(1)}, u32[]{:S(2)}, u32[]{:S(2)}) collective-permute-start(bf16[224,384]{1,0:T(8,128)(2,1)} %get-tuple-element.225), channel_id=1, source_target_pairs={{0,16},{8,24},{16,0},{24,8},{1,17},{9,25},{17,1},{25,9},{2,18},{10... | collective-permute-start | bytes 516104 | tf_op jit(solution)/shard_map/ppermute | solution.py:76
  (77 other events, 629.7 us)
Sparse Core Ops, SparseCore 0:
  144.1 55.0 reduce-scatter.2
  257.7 27.8 reduce-scatter.4
  287.4 33.2 all-gather.1
where the time goes:
time: 343 us; the launch traced here: 339 us
  Pallas kernels  185 us (54%)
  waiting for transfers between devices  61.1 us (18%)
  starting transfers between devices  52.8 us (15%)
  local copies, waits for them, and re-layouts  21.4 us (6%)
  between operations  14.7 us (4%)
  other arithmetic  4.01 us (1%)
    pallas_call x19, Pallas kernels, call(): pl.pallas_call(functools.partial(kernel, **fixed) if fixed else kernel, g...  180 us
    ppermute x41, waiting for transfers between devices, to_rep(): return lax.ppermute(array, 'rep', [(i, i ^ bit) for i in range(size)])  37.2 us
    ppermute x41, starting transfers between devices, to_rep(): return lax.ppermute(array, 'rep', [(i, i ^ bit) for i in range(size)])  32.2 us
    ppermute x11, waiting for transfers between devices, to_grp(): return lax.ppermute(array, 'grp', [(i, i ^ bit) for i in range(size)])  23.9 us
    ppermute x11, starting transfers between devices, to_grp(): return lax.ppermute(array, 'grp', [(i, i ^ bit) for i in range(size)])  20.5 us
    unnamed x104, local copies, waits for them, and re-layouts  11.4 us
  transfers between devices with their start and end apart: 55, of which 19 were waited for; matrix products, arithmetic and copies ran while one was open for 4% of the time, Pallas kernels for 46%

commit v1 on v0

v1 whole, which is shorter than its diff:
```python
import functools

import jax
import jax.numpy as jnp
from jax import lax
from jax.experimental import pallas as pl
from jax.experimental.pallas import tpu as pltpu
from jax.sharding import PartitionSpec as P

H = 12
HD = 64
EPSILON = 1e-06
MASKED = -1e30
DENSITY = 0.3989422804014327
ROOT_HALF = 0.7071067811865476

f32 = jnp.float32
bf16 = jnp.bfloat16
VMEM = pl.BlockSpec(memory_space=pltpu.VMEM)
SMEM = pl.BlockSpec(memory_space=pltpu.SMEM)
ANY = pl.BlockSpec(memory_space=pl.ANY)
VMEM_LIMIT = 63 * 2**20
COLS = 384
WEIGHT = 20
LOCAL = 8


def dot(a, b):
    return jnp.dot(a, b, preferred_element_type=f32)


def nt(a, b):
    return lax.dot_general(a, b, (((1,), (1,)), ((), ())), preferred_element_type=f32)


def tn(a, b):
    return lax.dot_general(a, b, (((0,), (0,)), ((), ())), preferred_element_type=f32)


def shape(dims, dtype):
    return jax.ShapeDtypeStruct(dims, dtype)


def al(value, by):
    return pl.multiple_of(value, by)


def call(kernel, outs, args, specs, out_specs, scratch=(), grid=(), flops=0, moved=0, aliases=None, **fixed):
    return pl.pallas_call(
        functools.partial(kernel, **fixed) if fixed else kernel,
        grid=grid,
        out_shape=outs,
        in_specs=specs,
        out_specs=out_specs,
        scratch_shapes=scratch,
        input_output_aliases=aliases or {},
        compiler_params=pltpu.CompilerParams(vmem_limit_bytes=VMEM_LIMIT),
        cost_estimate=pl.CostEstimate(
            flops=WEIGHT * flops, bytes_accessed=WEIGHT * moved, transcendentals=0
        ),
        name=kernel.__name__,
    )(*args)


def after(values, *events):
    return lax.optimization_barrier((values, events))[0]


def to_rep(array, bit):
    size = lax.axis_size("rep")
    return lax.ppermute(array, "rep", [(i, i ^ bit) for i in range(size)])


def to_grp(array, bit):
    size = lax.axis_size("grp")
    return lax.ppermute(array, "grp", [(i, i ^ bit) for i in range(size)])


def position():
    z = lax.axis_index("grp").astype(jnp.int32)
    p = lax.axis_index("rep").astype(jnp.int32) % LOCAL
    return jnp.stack([z, (p // 2) % 2, p // 4, p % 2, p])


class Copies:
    def __init__(self, sems):
        self.sems, self.held = sems, []

    def add(self, src, dst):
        copy = pltpu.make_async_copy(src, dst, self.sems.at[len(self.held)])
        copy.start()
        self.held.append(copy)

    def wait(self):
        for copy in self.held:
            copy.wait()


def piece_refs(kind, ref, zone, p, depth):
    if kind == "tall":
        rows = depth // LOCAL
        start = al(zone * depth + p * rows, 16)
        return [
            (ref.at[pl.ds(start, rows), pl.ds(half * COLS, COLS)], rows) for half in range(2)
        ]
    if kind == "wide":
        rows = depth // 2
        start = al(zone * depth + (p % 2) * rows, 16)
        return [
            (
                ref.at[pl.ds(start, rows), pl.ds(al((p // 2) * 2 * COLS + half * COLS, 128), COLS)],
                rows,
            )
            for half in range(2)
        ]
    if kind == "half":
        rows = depth // 2
        start = al(zone * depth + (p % 2) * rows, 16)
        return [(ref.at[pl.ds(start, rows), pl.ds(al((p // 2) * COLS, 128), COLS)], rows)]
    rows = depth // 4
    offset = int(kind)
    start = al(zone * depth + (p // 2) * rows, 16)
    return [(ref.at[pl.ds(start, rows), pl.ds(al(offset + (p % 2) * COLS, 128), COLS)], rows)]


def own_slab(ref, zone, depth, first=0, width=None):
    width = ref.shape[1] if width is None else width
    return ref.at[pl.ds(al(zone * depth, 16), depth), pl.ds(first, width)]


def block_rows(parts):
    return sum(rows for kind, ref, depth in parts for _, rows in piece_refs(kind, ref, 0, 0, depth))


def fetch(copies, pos, parts, held):
    zone, p = pos[0], pos[4]
    groups = lax.axis_size("grp")
    side = len(held) // 2
    n = held[0].shape[0] // (groups - 1) // (4 // side)
    for sib in range(2):
        for other in range(4):
            owner = p ^ (other * 2) ^ sib
            part = held[side * sib + other % side]
            at = 0 if side == 4 else other * (groups - 1) * n
            for step in range(1, groups):
                source = zone ^ step
                skip = at + n
                for kind, ref, depth in parts:
                    for place, rows in piece_refs(kind, ref, source, owner, depth):
                        copies.add(part.at[pl.ds(at, rows), :], place)
                        at += rows
                at = skip


def emit(copies, pos, parts, send, keep, quads=range(4), base=0, zones=None):
    core = pos[3]
    zones = range(lax.axis_size("grp")) if zones is None else zones
    for held, flip in ((send, 1), (keep, 0)):
        for zone in zones:
            for q in quads:
                owner = q * 2 + (core ^ flip)
                at = base
                for kind, ref, depth in parts:
                    for place, rows in piece_refs(kind, ref, zone, owner, depth):
                        copies.add(place, held.at[zone, q, pl.ds(at, rows), :])
                        at += rows


def add_first(pos, keep, got, sa, ka, sb, kb, kept, gotten, oa, pa, ob, pb, sems, out_sems):
    x, y = pos[1], pos[2]
    groups = keep.shape[0]
    half = groups // 2
    loads = [Copies(sems.at[zone]) for zone in range(groups)]
    for zone, load in enumerate(loads):
        load.add(keep.at[zone], kept.at[zone])
        load.add(got.at[zone], gotten.at[zone])
    stores = Copies(out_sems)
    for zone, load in enumerate(loads):
        load.wait()
        if zone < half:
            places = [(oa, j, j * 2 + (1 - x)) for j in range(2)] + [(pa, j, j * 2 + x) for j in range(2)]
            pairs = ((oa, sa), (pa, ka))
        else:
            places = [(ob, j, (1 - y) * 2 + j) for j in range(2)] + [(pb, j, y * 2 + j) for j in range(2)]
            pairs = ((ob, sb), (pb, kb))
        at = zone % half
        for ref, j, q in places:
            ref[at, j] = kept[zone, q] + gotten[zone, q]
        for ref, out in pairs:
            stores.add(ref.at[at], out.at[at])
    stores.wait()


def add_second(pos, ka, ra, kb, rb, sa, ja, sb, jb):
    x, y = pos[1], pos[2]
    for zone in range(ka.shape[0]):
        for kept, got, send, hold, at in ((ka, ra, sa, ja, y), (kb, rb, sb, jb, x)):
            send[zone] = kept[zone, 1 - at] + got[zone, 1 - at]
            hold[zone] = kept[zone, at] + got[zone, at]


def add_third(pos, ka, ra, kb, rb, *rest):
    outs, total = rest[:-1], rest[-1]
    half = ka.shape[0]
    for zone in range(half):
        total[zone] = ka[zone] + ra[zone]
        total[half + zone] = kb[zone] + rb[zone]
    for step, out in enumerate(outs):
        out[...] = total[pos[0] ^ step]


def add_fourth(*refs):
    total = refs[0][...].astype(f32)
    for ref in refs[1:-1]:
        total = total + ref[...].astype(f32)
    refs[-1][...] = total.astype(bf16)


def over_blocks(total):
    bit = LOCAL
    while bit < lax.axis_size("rep"):
        other = to_rep(total, bit)
        total = call(add_fourth, shape(total.shape, bf16), (total, other), [VMEM] * 2, VMEM)
        bit *= 2
    return total


class Reduce:
    def __init__(self, pos, send, keep):
        self.pos, self.keep = pos, keep
        self.n = keep.shape[2]
        self.size = keep.shape[0] * 4 * self.n * COLS * 2
        self.got = to_rep(send, 1)

    def one(self, *events):
        groups = self.keep.shape[0]
        quad = shape((groups // 2, 2, self.n, COLS), bf16)
        got = after(self.got, *events)
        block = pltpu.VMEM(self.keep.shape, bf16)
        part = pltpu.VMEM(quad.shape, bf16)
        sa, self.ka, sb, self.kb = call(
            add_first,
            (quad,) * 4,
            (self.pos, self.keep, got),
            [SMEM, ANY, ANY],
            (ANY,) * 4,
            scratch=[block, block, part, part, part, part]
            + [pltpu.SemaphoreType.DMA((groups, 2)), pltpu.SemaphoreType.DMA((2 * groups,))],
            moved=3 * self.size,
        )
        self.ra, self.rb = to_rep(sa, 2), to_rep(sb, 4)
        return self.ka

    def two(self, *events):
        pair = shape((self.ka.shape[0], self.n, COLS), bf16)
        ra, rb = after((self.ra, self.rb), *events)
        sa, self.ja, sb, self.jb = call(
            add_second,
            (pair,) * 4,
            (self.pos, self.ka, ra, self.kb, rb),
            [SMEM] + [VMEM] * 4,
            (VMEM,) * 4,
            moved=3 * self.size // 2,
        )
        self.ra, self.rb = to_rep(sa, 4), to_rep(sb, 2)
        return self.ja

    def three(self, *events):
        groups = self.keep.shape[0]
        ra, rb = after((self.ra, self.rb), *events)
        self.blocks = call(
            add_third,
            (shape((self.n, COLS), bf16),) * groups,
            (self.pos, self.ja, ra, self.jb, rb),
            [SMEM] + [VMEM] * 4,
            (VMEM,) * groups,
            scratch=[pltpu.VMEM((groups, self.n, COLS), bf16)],
            moved=3 * self.size // 4,
        )
        self.arrived = [to_grp(self.blocks[step], step) for step in range(1, groups)]
        return self.blocks[0]

    def four(self, *events):
        arrived = after(self.arrived, *events)
        total = call(
            add_fourth,
            shape((self.n, COLS), bf16),
            (self.blocks[0], *arrived),
            [VMEM] * (1 + len(arrived)),
            VMEM,
            moved=self.size // 3,
        )
        self.total = over_blocks(total)
        return self.total

    def around(self):
        self.near = [to_rep(self.total, bit) for bit in (2, 4, 6)]

    def five(self, *events):
        near = after(self.near, *events)
        held = jnp.concatenate([self.total, *near], axis=0)
        self.both = held, to_rep(held, 1)
        return held


def cut_first(pos, wq, wk, wv, wd, first, third):
    quarter, tall = wq.shape[0], wd.shape[0]
    for m, ref in enumerate((wq, wk, wv)):
        first[m * quarter : (m + 1) * quarter, :] = ref[...]
    for j in range(2):
        third[j * tall : (j + 1) * tall, :] = wd[:, j * COLS : (j + 1) * COLS]


def cut_more(pos, wo, wu, small, second):
    half, quarter = wu.shape[0], wo.shape[0]
    for j in range(2):
        second[j * half : (j + 1) * half, :] = wu[:, j * COLS : (j + 1) * COLS]
    second[2 * half : 2 * half + quarter, :] = wo[...]
    second[2 * half + quarter :, :] = small[...]


def join(*refs, counts):
    first = 0
    for count, out in zip(counts, refs[-len(counts) :]):
        at = 0
        for ref in refs[first : first + count]:
            out[at : at + ref.shape[0], :] = ref[...]
            at += ref.shape[0]
        first += count


def joined(*lists):
    blocks = [block for one in lists for block in one]
    return call(
        join,
        tuple(shape((sum(block.shape[0] for block in one), COLS), bf16) for one in lists),
        blocks,
        [VMEM] * len(blocks),
        (VMEM,) * len(lists),
        moved=sum(block.shape[0] for block in blocks) * COLS * 4,
        counts=tuple(len(one) for one in lists),
    )


def layer_norm(values):
    centred = values - jnp.mean(values, axis=-1, keepdims=True)
    spread_of = jnp.mean(centred * centred, axis=-1, keepdims=True)
    inverse = lax.rsqrt(spread_of + EPSILON)
    return centred * inverse, inverse


def norm_back(upstream, normed, inverse, gain):
    scaled = upstream * gain
    return inverse * (
        scaled
        - jnp.mean(scaled, axis=-1, keepdims=True)
        - normed * jnp.mean(scaled * normed, axis=-1, keepdims=True)
    )


def attend_heads(lengths, x, vectors, weight, q_out, k_out, v_out, mixed, logsum, pair):
    width = x.shape[1]
    rows = x[...]
    scaling = HD ** (-0.5)
    q_out[...] = (
        (dot(rows, weight[:, :width]) + vectors[0:1, :]).astype(bf16).astype(f32) * scaling
    ).astype(bf16)
    k_out[...] = dot(rows, weight[:, width : 2 * width]).astype(bf16)
    v_out[...] = (dot(rows, weight[:, 2 * width :]) + vectors[1:2, :]).astype(bf16)
    slots = rows.shape[0]
    lane = lax.broadcasted_iota(jnp.int32, (slots, 128), 1)
    low = lane < HD
    slot = lax.broadcasted_iota(jnp.int32, (1, slots), 1)
    bias = jnp.where(slot < lengths[pair], 0.0, MASKED).astype(f32)

    def heads(h, sums):
        s = pl.ds(al(h * 128, 128), 128)
        q1, k1, v1 = q_out[:, s], k_out[:, s], v_out[:, s]
        results, peaks = [], []
        for e in range(2):
            mask = low if e == 0 else ~low
            scores = nt(jnp.where(mask, q1, 0).astype(bf16), k1) + bias
            peak = jnp.max(scores, axis=1, keepdims=True)
            expo = jnp.exp(scores - peak).astype(bf16)
            results.append(dot(expo, jnp.where(mask, v1, 1).astype(bf16)))
            peaks.append(peak)
        total = pltpu.roll(jnp.where(low, results[1], results[0]), HD, 1)
        mixed[:, s] = (jnp.where(low, results[0], results[1]) / total).astype(bf16)
        sums = jnp.where(lane % HD == h, jnp.where(low, peaks[0], peaks[1]) + jnp.log(total), sums)
        return sums

    sums = lax.fori_loop(0, H // 2, heads, jnp.zeros((slots, 128), f32), unroll=True)
    turned = sums.T
    logsum[0, :8] = turned[:8]
    logsum[0, 8:] = turned[HD : HD + 8]


def attend(pos, lengths, x, wq, wk, wv, vectors, *rest):
    held, (q_out, k_out, v_out, mixed, logsum, w_out, weight, sems) = rest[:2], rest[2:]
    depth, width = wq.shape
    pair = pl.program_id(0)
    write = pltpu.make_async_copy(weight, w_out, sems.at[sems.shape[0] - 1])

    @pl.when(pair == 0)
    def _():
        copies = Copies(sems)
        for m, ref in enumerate((wq, wk, wv)):
            copies.add(ref, own_slab(weight, pos[0], depth, m * width, width))
        fetch(copies, pos, [(str(m * width), weight, depth) for m in range(3)], held)
        copies.wait()
        write.start()

    attend_heads(lengths, x, vectors, weight, q_out, k_out, v_out, mixed, logsum, pair)

    @pl.when(pair == pl.num_programs(0) - 1)
    def _():
        write.wait()


def expand_rows(x, mixed, vectors, up_bias, up, out_w, act, slope, normed, inverse):
    first = x[...].astype(f32) + dot(mixed[...], out_w[...]) + vectors[2:3, :]
    normal, scale = layer_norm(first)
    normed[...] = normal
    inverse[...] = jnp.broadcast_to(scale, inverse.shape)
    hidden = (normal * vectors[3:4, :] + vectors[4:5, :]).astype(bf16)
    chunk = 768
    for j in range(up.shape[1] // chunk):
        s = slice(j * chunk, (j + 1) * chunk)
        u = dot(hidden, up[:, s]) + up_bias[:, s]
        cdf, pdf = gaussian(u)
        act[:, s] = (u * cdf).astype(bf16)
        slope[:, s] = (cdf + u * pdf).astype(bf16)


def expand(pos, x, mixed, wu, wo, vectors, up_bias, *rest):
    held, (act, slope, normed, inverse, wu_out, wo_out, up, out_w, sems) = rest[:8], rest[8:]
    step = pl.program_id(0)
    depth = wo.shape[0]
    last = sems.shape[0]
    writes = [
        pltpu.make_async_copy(up, wu_out, sems.at[last - 1]),
        pltpu.make_async_copy(out_w, wo_out, sems.at[last - 2]),
    ]

    @pl.when(step == 0)
    def _():
        copies = Copies(sems)
        copies.add(wu, own_slab(up, pos[0], depth))
        copies.add(wo, own_slab(out_w, pos[0], depth))
        fetch(copies, pos, [("wide", up, depth), ("0", out_w, depth)], held)
        copies.wait()
        for write in writes:
            write.start()

    expand_rows(x, mixed, vectors, up_bias, up, out_w, act, slope, normed, inverse)

    @pl.when(step == pl.num_programs(0) - 1)
    def _():
        for write in writes:
            write.wait()


def gaussian(u):
    return 0.5 + 0.5 * lax.erf(u * ROOT_HALF), jnp.exp(-0.5 * u * u) * DENSITY


def feed_forward(pos, lengths, act, slope, normed, inverse, cotangent, mixed, wd, wu, wo, vectors, *rest):
    held, rest = rest[:8], rest[8:]
    output, grad_first, grad_mixed, down_send, down_keep, send, keep = rest[:7]
    down, acts, expos, hiddens, lows, lows_first, grad_out, last_sums, first_sums, up_sums, blocks = rest[7:18]
    up, out_w, mixes, sems, act_sems, out_sems, late_sems = rest[18:]
    step = pl.program_id(0)
    steps = pl.num_programs(0) - 1
    depth = wd.shape[0]
    rows, width = normed.shape

    def part(i):
        return pltpu.make_async_copy(
            act.at[pl.ds(al(i * rows, 16), rows), :],
            acts.at[pl.ds(al(i * rows, 16), rows), :],
            act_sems.at[i],
        )

    def late(i):
        return pltpu.make_async_copy((wu, wo, mixed)[i], (up, out_w, mixes)[i], late_sems.at[i])

    @pl.when(step == 0)
    def _():
        copies = Copies(sems)
        copies.add(wd, own_slab(down, pos[0], depth))
        fetch(copies, pos, [("tall", down, depth)], held)
        for i in range(act_sems.shape[0]):
            part(i).start()
        for i in range(3):
            late(i).start()
        copies.wait()
        late(0).wait()
        late(1).wait()
        last_sums[...] = jnp.zeros_like(last_sums)
        first_sums[...] = jnp.zeros_like(first_sums)
        up_sums[...] = jnp.zeros_like(up_sums)

    @pl.when(step < steps)
    def _():
        part(step).wait()
        s = pl.ds(al(step * rows, 16), rows)
        per_pair = acts.shape[0] // lengths.shape[0] // rows
        slot = lax.broadcasted_iota(jnp.int32, (rows, 1), 0) + lax.rem(step, per_pair) * rows
        mask = (slot < lengths[step // per_pair]).astype(f32)
        first_normal = normed[...]
        first_gain = vectors[3:4, :]
        hidden = first_normal * first_gain + vectors[4:5, :]
        hiddens[s, :] = hidden.astype(bf16)
        second = hidden + dot(acts[s, :], down[...]) + vectors[5:6, :]
        normal, scale = layer_norm(second)
        gain = vectors[6:7, :]
        output[...] = ((normal * gain + vectors[7:8, :]) * mask).astype(bf16)
        upstream = cotangent[...].astype(f32) * mask
        grad_second = norm_back(upstream, normal, scale, gain)
        low = grad_second.astype(bf16)
        lows[s, :] = low
        last_sums[0:1, :] += jnp.sum(upstream * normal, axis=0, keepdims=True)
        last_sums[1:2, :] += jnp.sum(upstream, axis=0, keepdims=True)
        last_sums[2:3, :] += jnp.sum(low.astype(f32), axis=0, keepdims=True)
        chunk = 768
        for j in range(expos.shape[1] // chunk):
            c = slice(j * chunk, (j + 1) * chunk)
            grown = (nt(low, down[c, :]) * slope[:, c].astype(f32)).astype(bf16)
            expos[s, c] = grown
            up_sums[0:1, c] += jnp.sum(grown.astype(f32), axis=0, keepdims=True)
        upstream = grad_second + nt(expos[s, :], up[...])
        result = norm_back(upstream, first_normal, inverse[:, 0:1], first_gain)
        grad_first[...] = result
        low = result.astype(bf16)
        lows_first[s, :] = low
        grad_mixed[...] = nt(low, out_w[...]).astype(bf16)
        first_sums[0:1, :] += jnp.sum(upstream * first_normal, axis=0, keepdims=True)
        first_sums[1:2, :] += jnp.sum(upstream, axis=0, keepdims=True)
        first_sums[2:3, :] += jnp.sum(low.astype(f32), axis=0, keepdims=True)

    @pl.when(step == steps)
    def _():
        copies = Copies(out_sems)
        for zone in range(down.shape[0] // depth):
            s = slice(zone * depth, (zone + 1) * depth)
            down[s, :] = tn(acts[:, s], lows[...]).astype(bf16)
            emit(copies, pos, [("tall", down, depth)], down_send, down_keep, zones=(zone,))
        grad_up = acts.at[pl.ds(0, width), :]
        up_depth = width // lax.axis_size("grp")
        chunk = 2 * COLS
        for j in range(acts.shape[1] // chunk):
            c = slice(j * chunk, (j + 1) * chunk)
            acts[:width, c] = tn(hiddens[...], expos[:, c]).astype(bf16)
            emit(copies, pos, [("wide", grad_up, up_depth)], send, keep, (j,))
        late(2).wait()
        grad_out[...] = tn(mixes[...], lows_first[...]).astype(bf16)
        emit(copies, pos, [("0", grad_out, up_depth)], send, keep, base=up_depth)
        vector_blocks(
            blocks,
            [last_sums[i : i + 1, :] for i in range(3)]
            + [up_sums[0:1, j * width : (j + 1) * width] for j in range(4)]
            + [first_sums[i : i + 1, :] for i in range(3)],
        )
        emit_vectors(copies, pos, blocks, up_depth + up_depth // 4, send, keep)
        copies.wait()


def vector_blocks(blocks, rows):
    blocks[...] = jnp.zeros_like(blocks)
    for p in range(min(LOCAL, len(rows))):
        here = rows[p::LOCAL]
        half = here[0].shape[1] // 2
        stacked = [part for row in here for part in (row[:, :half], row[:, half:])]
        stacked.append(jnp.zeros((16 - 2 * len(here), half), f32))
        blocks[p] = jnp.concatenate(stacked, axis=0).astype(bf16)


def vector_of(block, i):
    at = 2 * (i // LOCAL)
    return jnp.concatenate([block[at : at + 1, :], block[at + 1 : at + 2, :]], axis=1)


def emit_vectors(copies, pos, blocks, base, send, keep):
    for held, flip in ((send, 1), (keep, 0)):
        for zone in range(send.shape[0]):
            for q in range(4):
                owner = q * 2 + (pos[3] ^ flip)
                copies.add(blocks.at[owner], held.at[zone, q, pl.ds(base, 16), :])


def pair_back(lengths, q, k, v, mixed, grad_mixed, logsum, *rest, pair):
    if pair:
        old_sums, rest = rest[0], rest[2:]
    grads, sums, rows_of, held, deltas, in_sems, out_sem = rest
    slots, width = held.shape[0], q.shape[1]
    here = pl.ds(pair * slots, slots)
    copies = Copies(in_sems)
    for i, ref in enumerate((mixed, grad_mixed, q, k, v)):
        copies.add(ref.at[here, :], rows_of.at[i])
    sums[...] = old_sums[...] if pair else jnp.zeros_like(sums)
    low = lax.broadcasted_iota(jnp.int32, (slots, 128), 1) < HD
    slot = lax.broadcasted_iota(jnp.int32, (slots, 1), 0)
    select = (
        lax.broadcasted_iota(jnp.int32, (16, width), 1) // HD
        == lax.broadcasted_iota(jnp.int32, (16, width), 0)
    ).astype(bf16)
    scaling = HD ** (-0.5)
    bias = jnp.where(slot < lengths[pair], 0.0, MASKED).astype(f32)
    copies.wait()
    product = rows_of[0].astype(f32) * rows_of[1].astype(f32)
    high = product.astype(bf16)
    rest_of = (product - high.astype(f32)).astype(bf16)
    deltas[...] = nt(select, high) + nt(select, rest_of)

    def heads(h, carry):
        s = pl.ds(al(h * 128, 128), 128)
        g1, q1, k1, v1 = (rows_of[i, :, s] for i in (1, 2, 3, 4))
        probs, scores_back, qs, gs, ks = [], [], [], [], []
        for e in range(2):
            mask = low if e == 0 else ~low
            qm = jnp.where(mask, q1, 0).astype(bf16)
            gm = jnp.where(mask, g1, 0).astype(bf16)
            prob = jnp.exp(nt(k1, qm) + bias - logsum[pair, pl.ds(h + 8 * e, 1), :])
            back = prob * (nt(v1, gm) - deltas[pl.ds(h * 2 + e, 1), :])
            probs.append(prob.astype(bf16))
            scores_back.append(back.astype(bf16))
            qs.append(qm)
            gs.append(gm)
            ks.append(jnp.where(mask, k1, 0).astype(bf16))
        grad_v = dot(jnp.concatenate(probs, 1), jnp.concatenate(gs, 0))
        grad_k = dot(jnp.concatenate(scores_back, 1), jnp.concatenate(qs, 0))
        grad_q = tn(jnp.concatenate(scores_back, 0), jnp.concatenate(ks, 0)) * scaling
        for m, value in enumerate((grad_q, grad_k, grad_v)):
            value = value.astype(bf16)
            held[:, pl.ds(al(m * width + h * 128, 128), 128)] = value
            if m != 1:
                sums[m : m + 1, s] += jnp.sum(value.astype(f32), axis=0, keepdims=True)
        return carry

    lax.fori_loop(0, H // 2, heads, 0, unroll=True)
    store = pltpu.make_async_copy(held, grads.at[here, :], out_sem.at[0])
    store.start()
    store.wait()


def heads_weights(pos, x, grads, sums, send, keep, xs, held, weight_grads, blocks, sems, out_sems):
    width = xs.shape[1]
    depth = width // lax.axis_size("grp")
    copies = Copies(sems)
    copies.add(x, xs)
    for m in range(3):
        c = pl.ds(m * width, width)
        copies.add(grads.at[:, c], held.at[:, c])
    copies.held[0].wait()
    stores = Copies(out_sems)
    vector_blocks(blocks, [sums[m : m + 1, :] for m in (0, 2)])
    emit_vectors(stores, pos, blocks, 3 * depth // 4, send, keep)
    for m in range(3):
        c = slice(m * width, (m + 1) * width)
        copies.held[1 + m].wait()
        weight_grads[:, c] = tn(xs[...], held[:, c]).astype(bf16)
        emit(stores, pos, [(str(m * width), weight_grads, depth)], send, keep, base=m * depth // 4)
    stores.wait()


def inputs_back(grad_first, grads, weight, out):
    out[...] = (grad_first[...] + nt(grads[...], weight[...])).astype(bf16)


def place_ffn(pos, mine, sibling, gd, gu, go, g2, s2, bd, bu, g1, s1, bo, small):
    tall, half, quarter = gd.shape[0] // LOCAL, gu.shape[0] // 2, go.shape[0] // 4
    n = mine.shape[0] // 4 - 2 * tall
    for sib, held in ((0, mine), (1, sibling)):
        for other in range(4):
            owner = pos[4] ^ (other * 2) ^ sib
            at = other * 2 * tall
            for j in range(2):
                gd[pl.ds(al(owner * tall, 16), tall), j * COLS : (j + 1) * COLS] = held[
                    at : at + tall, :
                ].astype(f32)
                at += tall
            at = 8 * tall + (0, 2, 1, 3)[other] * n
            for j in range(2):
                first = pl.ds(al((owner // 2) * 2 * COLS + j * COLS, 128), COLS)
                gu[pl.ds(al((owner % 2) * half, 16), half), first] = held[at : at + half, :].astype(f32)
                at += half
            rows = pl.ds(al((owner // 2) * quarter, 16), quarter)
            go[rows, pl.ds(al((owner % 2) * COLS, 128), COLS)] = held[at : at + quarter, :].astype(f32)
            at += quarter
            small[owner] = held[at : at + 16, :].astype(f32)

    for i, out in ((0, g2), (1, s2), (2, bd), (7, g1), (8, s1), (9, bo)):
        out[...] = own_part(pos, vector_of(small[i % LOCAL], i), out.shape[1])
    total = jnp.zeros(bu.shape, f32)
    for zone in range(4):
        total = jnp.where(pos[0] == zone, vector_of(small[3 + zone], 3 + zone), total)
    bu[...] = total


def own_part(pos, row, size):
    total = row[:, :size]
    for zone in range(1, row.shape[1] // size):
        total = jnp.where(pos[0] == zone, row[:, zone * size : (zone + 1) * size], total)
    return total


def place_heads(pos, mine, sibling, gq, gk, gv, bq, bv, small):
    quarter = gq.shape[0] // 4
    n = mine.shape[0] // 4
    for sib, held in ((0, mine), (1, sibling)):
        for other in range(4):
            owner = pos[4] ^ (other * 2) ^ sib
            row4 = pl.ds(al((owner // 2) * quarter, 16), quarter)
            col2 = pl.ds(al((owner % 2) * COLS, 128), COLS)
            at = other * n
            for out in (gq, gk, gv):
                out[row4, col2] = held[at : at + quarter, :].astype(f32)
                at += quarter
            small[owner] = held[at : at + 16, :].astype(f32)[:8]
    for i, out in enumerate((bq, bv)):
        out[...] = own_part(pos, vector_of(small[i], i), out.shape[1])


def shards(
    tokens,
    lengths,
    cotangent,
    query_weight,
    query_bias,
    key_weight,
    value_weight,
    value_bias,
    out_weight,
    out_bias,
    norm_gain,
    norm_shift,
    up_weight,
    up_bias,
    down_weight,
    down_bias,
    final_gain,
    final_shift,
):
    groups = lax.axis_size("grp")
    pairs, seqlen, width = tokens.shape
    rows = pairs * seqlen
    depth = width // groups
    wide = up_weight.shape[1]
    inputs = tokens.reshape(rows, width)
    upstream = cotangent.reshape(rows, width)
    pos = position()
    n1 = 3 * depth // 4
    n2 = depth + depth // 4
    n3 = depth

    def cut(kernel, sizes, args, specs):
        return pl.pallas_call(
            kernel,
            grid_spec=pltpu.PrefetchScalarGridSpec(
                num_scalar_prefetch=1,
                grid=(1,),
                in_specs=specs,
                out_specs=[pl.BlockSpec((n, COLS), lambda i, at: (0, 0)) for n in sizes],
            ),
            out_shape=[shape((n, COLS), bf16) for n in sizes],
            name=kernel.__name__,
        )(pos, *args)

    square = pl.BlockSpec((depth // 4, COLS), lambda i, at: (at[4] // 2, at[4] % 2))
    tall = pl.BlockSpec((down_weight.shape[0] // LOCAL, width), lambda i, at: (at[4], 0))
    first, third = cut(
        cut_first,
        (n1, n3),
        (query_weight, key_weight, value_weight, down_weight),
        [square] * 3 + [tall],
    )
    z1 = [to_grp(first, step) for step in range(1, groups)]
    close = to_grp(third, 1)
    small = jnp.concatenate(
        after(
            [
                query_bias,
                value_bias,
                out_bias,
                norm_gain,
                norm_shift,
                down_bias,
                final_gain,
                final_shift,
                up_bias,
            ],
            first,
        )
    )
    count = small.shape[0] // COLS
    small = jnp.pad(small.reshape(count, COLS), ((0, 16 - count), (0, 0)))
    (second,) = cut(
        cut_more,
        (n2 + 16,),
        (out_weight, up_weight, small),
        [
            square,
            pl.BlockSpec((depth // 2, 2 * COLS), lambda i, at: (at[4] % 2, at[4] // 2)),
            pl.BlockSpec((16, COLS), lambda i, at: (0, 0)),
        ],
    )
    z1 = after(z1, second)

    def near(mine):
        return [mine, *(to_rep(mine, bit) for bit in (2, 4, 6))]

    def other_core(held):
        return [to_rep(part, 1) for part in held]

    mine1 = jnp.concatenate(z1, axis=0)
    from_x, from_y = to_rep(mine1, 2), to_rep(mine1, 4)
    second = after(second, z1)
    far = [to_grp(second, 2), to_grp(second, 3)]
    cut_at = (mine1.shape[0] // 2 + 47) // 48 * 48
    low, high = to_rep(from_x[:cut_at], 4), to_rep(from_y[cut_at:], 2)
    parts = [second, to_grp(after(second, (from_x, from_y)), 1), *far]
    parts[1:] = after(parts[1:], (low, high))
    mine2 = jnp.concatenate([part[:n2] for part in parts[1:]], axis=0)
    held2 = near(mine2)
    held1 = jnp.concatenate([mine1, from_x, from_y, low, high], axis=0)
    held1 = [held1, to_rep(held1, 1)]
    flat = jnp.stack([part[n2 : n2 + count].reshape(-1) for part in parts])
    by_zone = jnp.stack([flat[pos[0] ^ zone] for zone in range(groups)]).astype(f32)
    vectors = by_zone[:, : 8 * depth].reshape(groups, 8, depth).transpose(1, 0, 2).reshape(8, width)
    up_vector = by_zone[:, 8 * depth :].reshape(1, wide)
    third, close = after((third, close), mine2)
    far = [to_grp(third, 2), to_grp(third, 3)]

    row_block = 256
    blocks_of = rows // row_block
    mat = shape((rows, width), bf16)
    mat32 = shape((rows, width), f32)
    dense = 2 * rows * width * width
    by_pair = pl.BlockSpec((seqlen, width), lambda i: (i, 0))
    q, k, v, mixed, logsum, w_all = call(
        attend,
        (mat, mat, mat, mat, shape((pairs, 16, seqlen), f32), shape((width, 3 * width), bf16)),
        (pos, lengths, after(inputs, (mine2, close)), query_weight, key_weight, value_weight, vectors, *held1),
        [SMEM, SMEM, by_pair, ANY, ANY, ANY, VMEM] + [ANY] * 2,
        (by_pair,) * 4 + (pl.BlockSpec((1, 16, seqlen), lambda i: (i, 0, 0)), ANY),
        scratch=[
            pltpu.VMEM((width, 3 * width), bf16),
            pltpu.SemaphoreType.DMA((4 + 8 * (groups - 1) * 3,)),
        ],
        grid=(pairs,),
        flops=12 * dense,
        moved=12 * rows * width,
    )
    held2, far = after((held2, far), w_all)
    held2 += other_core(held2)
    (mine3,) = joined((close, *far))
    held3 = near(mine3)
    held3 += other_core(held3[:1])
    by_row = pl.BlockSpec((row_block, width), lambda i: (i, 0))
    by_wide = pl.BlockSpec((row_block, wide), lambda i: (i, 0))
    by_lane = pl.BlockSpec((row_block, 128), lambda i: (i, 0))
    act, slope, normed, inverse, wu_all, wo_all = call(
        expand,
        (
            shape((rows, wide), bf16),
            shape((rows, wide), bf16),
            mat32,
            shape((rows, 128), f32),
            shape((width, wide), bf16),
            shape((width, width), bf16),
        ),
        (pos, after(inputs, held3[0]), mixed, up_weight, out_weight, vectors, up_vector, *held2),
        [SMEM, by_row, by_row, ANY, ANY, VMEM, VMEM] + [ANY] * 8,
        (by_wide, by_wide, by_row, by_lane, ANY, ANY),
        scratch=[
            pltpu.VMEM((width, wide), bf16),
            pltpu.VMEM((width, width), bf16),
            pltpu.SemaphoreType.DMA((4 + 8 * (groups - 1) * 3,)),
        ],
        grid=(blocks_of,),
        flops=8 * dense,
        moved=18 * rows * width,
    )
    held3 = after(held3, wo_all)
    held3 += other_core(held3[1:4])

    stay = lambda i: (jnp.minimum(i, blocks_of - 1), 0)
    by_row = pl.BlockSpec((row_block, width), stay)
    by_wide = pl.BlockSpec((row_block, wide), stay)
    by_lane = pl.BlockSpec((row_block, 128), stay)
    vec = shape((8, width), f32)
    vec_out = pl.BlockSpec((8, width), lambda i: (0, 0))

    def travelling(n):
        return (shape((groups, 4, n, COLS), bf16),) * 2

    n_up = depth + depth // 4 + 16
    output, grad_first, grad_mixed, down_send, down_keep, send, keep = call(
        feed_forward,
        (mat, mat32, mat, *travelling(n3), *travelling(n_up)),
        (pos, lengths, act, slope, normed, inverse, upstream, mixed, down_weight, wu_all, wo_all, vectors)
        + tuple(held3),
        [SMEM, SMEM, ANY, by_wide, by_row, by_lane, by_row, ANY, ANY, ANY, ANY, VMEM] + [ANY] * 8,
        (by_row, by_row, by_row, ANY, ANY, ANY, ANY),
        scratch=[
            pltpu.VMEM((wide, width), bf16),
            pltpu.VMEM((rows, wide), bf16),
            pltpu.VMEM((rows, wide), bf16),
            pltpu.VMEM((rows, width), bf16),
            pltpu.VMEM((rows, width), bf16),
            pltpu.VMEM((rows, width), bf16),
            pltpu.VMEM((width, width), bf16),
            pltpu.VMEM((8, width), f32),
            pltpu.VMEM((8, width), f32),
            pltpu.VMEM((8, wide), f32),
            pltpu.VMEM((LOCAL, 16, COLS), bf16),
            pltpu.VMEM((width, wide), bf16),
            pltpu.VMEM((width, width), bf16),
            pltpu.VMEM((rows, width), bf16),
            pltpu.SemaphoreType.DMA((4 + 8 * (groups - 1) * 2,)),
            pltpu.SemaphoreType.DMA((blocks_of,)),
            pltpu.SemaphoreType.DMA((groups * 4 * 2 * 6,)),
            pltpu.SemaphoreType.DMA((3,)),
        ],
        grid=(blocks_of + 1,),
        flops=22 * dense,
        moved=50 * rows * width,
    )
    down = Reduce(pos, down_send, down_keep)
    up = Reduce(pos, after(send, down.got), keep)
    done = down.one()
    done = up.one(done)

    n_heads = n1 + 16
    grads = sums = None
    for pair in range(pairs):
        grads, sums = call(
            pair_back,
            (shape((rows, 3 * width), bf16), vec),
            (lengths, q, k, v, mixed, grad_mixed, after(logsum, done))
            + ((sums, grads) if pair else ()),
            [SMEM] + [ANY] * 5 + [VMEM] + ([VMEM, ANY] if pair else []),
            (ANY, VMEM),
            scratch=[
                pltpu.VMEM((5, seqlen, width), bf16),
                pltpu.VMEM((seqlen, 3 * width), bf16),
                pltpu.VMEM((16, seqlen), f32),
                pltpu.SemaphoreType.DMA((5,)),
                pltpu.SemaphoreType.DMA((1,)),
            ],
            flops=12 * dense // pairs,
            moved=12 * rows * width,
            aliases={8: 0} if pair else None,
            pair=pair,
        )
        if pair == 0:
            done = down.two(grads)
    done = up.two(grads)
    done = down.three(done)
    send, keep = call(
        heads_weights,
        travelling(n_heads),
        (pos, after(inputs, done), grads, sums),
        [SMEM, ANY, ANY, VMEM],
        (ANY, ANY),
        scratch=[
            pltpu.VMEM((rows, width), bf16),
            pltpu.VMEM((rows, 3 * width), bf16),
            pltpu.VMEM((width, 3 * width), bf16),
            pltpu.VMEM((LOCAL, 16, COLS), bf16),
            pltpu.SemaphoreType.DMA((4,)),
            pltpu.SemaphoreType.DMA((groups * 4 * 2 * 4,)),
        ],
        flops=3 * dense,
        moved=12 * rows * width,
    )
    heads = Reduce(pos, after(send, (up.ra, up.rb, down.arrived)), keep)
    done = up.three(down.arrived)
    done = heads.one(done)
    by_row = pl.BlockSpec((row_block, width), lambda i: (i, 0))
    grad_inputs = call(
        inputs_back,
        mat,
        (after(grad_first, done), grads, w_all),
        [by_row, pl.BlockSpec((row_block, 3 * width), lambda i: (i, 0)), VMEM],
        by_row,
        grid=(blocks_of,),
        flops=3 * dense,
        moved=16 * rows * width,
    )
    done = heads.two(grad_inputs, up.arrived)
    down_total = down.four(done)
    up_total = up.four(down_total)
    down_total, up_total = after((down_total, up_total), (heads.ra, heads.rb))
    heads.three()
    near_down, near_up = after((to_rep(down_total, 2), to_rep(up_total, 4)), heads.blocks[0])
    down_pair, up_pair = joined((down_total, near_down), (up_total, near_up))
    (both,) = joined((down_pair, to_rep(down_pair, 4), up_pair, to_rep(up_pair, 2)))
    heads.four()
    heads.around()
    both = both, to_rep(after(both, heads.arrived), 1)
    vector = shape((1, depth), f32)
    square = shape((depth, width), f32)
    gd, gu, go, g2, s2, bd, bu, g1, s1, bo = call(
        place_ffn,
        (shape((wide // groups, width), f32), shape((depth, wide), f32), square)
        + (vector,) * 3
        + (shape((1, wide // groups), f32),)
        + (vector,) * 3,
        (pos, *both),
        [SMEM, VMEM, VMEM],
        (VMEM,) * 10,
        scratch=[pltpu.VMEM((LOCAL, 16, COLS), f32)],
        moved=24 * depth * width,
    )
    heads.five(gd)
    gq, gk, gv, bq, bv = call(
        place_heads,
        (square,) * 3 + (vector,) * 2,
        (pos, *heads.both),
        [SMEM] + [VMEM] * 2,
        (VMEM,) * 5,
        scratch=[pltpu.VMEM((LOCAL, 8, COLS), f32)],
        moved=24 * depth * width,
    )
    bq, bv, bo, g1, s1, bu, bd, g2, s2 = (
        row.reshape(-1) for row in (bq, bv, bo, g1, s1, bu, bd, g2, s2)
    )
    return (
        output.reshape(pairs, seqlen, width),
        grad_inputs.reshape(pairs, seqlen, width),
        gq,
        bq,
        gk,
        gv,
        bv,
        go,
        bo,
        g1,
        s1,
        gu,
        bu,
        gd,
        bd,
        g2,
        s2,
    )


def solution(mesh):
    pairs = P(("grp", "rep"), None, None)
    matrix = P("grp", None)
    vector = P("grp")
    placed = (pairs, P(("grp", "rep")), pairs, matrix, vector, matrix, matrix, vector, matrix, vector)
    placed += (vector, vector, matrix, vector, matrix, vector, vector, vector)
    results = (pairs, pairs, matrix, vector, matrix, matrix, vector, matrix, vector, vector, vector)
    results += (matrix, vector, matrix, vector, vector, vector)
    return jax.shard_map(shards, mesh=mesh, in_specs=placed, out_specs=results, check_vma=False)
```

time: 343 us -> 302 us (0.88)
  waiting for transfers between devices: 61.1 us -> 37.4 us
  between operations: 14.7 us -> 1.68 us
  local copies, waits for them, and re-layouts: 21.4 us -> 10.3 us
  starting transfers between devices: 52.8 us -> 60.6 us
    ppermute x41 -> x43, waiting for transfers between devices: 37.2 us -> 23.3 us  [to_rep(): return lax.ppermute(array, 'rep', [(i, i ^ bit) for i in range(size)])]
    ppermute x11 -> x18, waiting for transfers between devices: 23.9 us -> 14 us  [to_grp(): return lax.ppermute(array, 'grp', [(i, i ^ bit) for i in range(size)])]
    concatenate x1, local copies, waits for them, and re-layouts: 6.1 us -> 0.09 us  [shards(): jnp.concatenate(after([query_bias, value_bias, out_bias, norm_gain, norm_...]
    ppermute x11 -> x18, starting transfers between devices: 20.5 us -> 24.9 us  [to_grp(): return lax.ppermute(array, 'grp', [(i, i ^ bit) for i in range(size)])]
    unnamed x104 -> x92, local copies, waits for them, and re-layouts: 11.4 us -> 7.95 us
    ppermute x41 -> x43, starting transfers between devices: 32.2 us -> 35.6 us  [to_rep(): return lax.ppermute(array, 'rep', [(i, i ^ bit) for i in range(size)])]
    pallas_call x19 -> x24, Pallas kernels: 180 us -> 182 us  [call(): pl.pallas_call(functools.partial(kernel, **fixed) if fixed else kernel, g...]
  transfers between devices with their start and end apart: 55 -> 61, of which waited for: 19 -> 22; matrix products, arithmetic and copies ran while one was open for 4% -> 2% of each run, Pallas kernels for 46% -> 42%
where the time goes in v1:
time: 302 us; the launch traced here: 298 us
  Pallas kernels  186 us (62%)
  starting transfers between devices  60.6 us (20%)
  waiting for transfers between devices  37.4 us (12%)
  local copies, waits for them, and re-layouts  10.3 us (3%)
    pallas_call x24, Pallas kernels, call(): pl.pallas_call(functools.partial(kernel, **fixed) if fixed else kernel, g...  182 us
    ppermute x43, starting transfers between devices, to_rep(): return lax.ppermute(array, 'rep', [(i, i ^ bit) for i in range(size)])  35.6 us
    ppermute x18, starting transfers between devices, to_grp(): return lax.ppermute(array, 'grp', [(i, i ^ bit) for i in range(size)])  24.9 us
    ppermute x43, waiting for transfers between devices, to_rep(): return lax.ppermute(array, 'rep', [(i, i ^ bit) for i in range(size)])  23.3 us
    ppermute x18, waiting for transfers between devices, to_grp(): return lax.ppermute(array, 'grp', [(i, i ^ bit) for i in range(size)])  14 us
    unnamed x92, local copies, waits for them, and re-layouts  7.95 us
  transfers between devices with their start and end apart: 61, of which 22 were waited for; matrix products, arithmetic and copies ran while one was open for 2% of the time, Pallas kernels for 42%

profile of v1, /device:TPU:0, one launch (start us, length us, event | category | flops | bytes accessed | tf_op | source)
XLA Modules:
  0.0 298.5 jit_solution(13112839809831876459)
XLA Ops:
  1.5 2.3 cut_first.1
  3.8 5.0 %collective-permute-start.3 = (bf16[144,384]{1,0:T(8,128)(2,1)}, bf16[144,384]{1,0:T(8,128)(2,1)S(1)}, u32[]{:S(2)}, u32[]{:S(2)}) collective-permute-start(bf16[144,384]{1,0:T(8,128)(2,1)} %get-tuple-element.167), channel_id=1, source_target_pairs={{0,24},{8,16},{16,8},{24,0},{1,25},{9,17},{17,9},{25,1},{2,26},{10... | collective-permute-start | bytes 331784 | tf_op jit(solution)/shard_map/ppermute | solution.py:76
  10.2 2.3 cut_more.1
  13.0 5.3 %collective-permute-done.2 = bf16[144,384]{1,0:T(8,128)(2,1)S(1)} collective-permute-done((bf16[144,384]{1,0:T(8,128)(2,1)}, bf16[144,384]{1,0:T(8,128)(2,1)S(1)}, u32[]{:S(2)}, u32[]{:S(2)}) %collective-permute-start.2) | collective-permute-done | bytes 110624 | tf_op jit(solution)/shard_map/ppermute | solution.py:76
  30.7 3.9 %collective-permute-done.9 = bf16[240,384]{1,0:T(8,128)(2,1)S(1)} collective-permute-done((bf16[240,384]{1,0:T(8,128)(2,1)S(1)}, bf16[240,384]{1,0:T(8,128)(2,1)S(1)}, u32[]{:S(2)}, u32[]{:S(2)}) %collective-permute-start.9) | collective-permute-done | bytes 184352 | tf_op jit(solution)/shard_map/ppermute | solution.py:71
  35.0 6.1 %collective-permute-done.7 = bf16[256,384]{1,0:T(8,128)(2,1)S(1)} collective-permute-done((bf16[256,384]{1,0:T(8,128)(2,1)}, bf16[256,384]{1,0:T(8,128)(2,1)S(1)}, u32[]{:S(2)}, u32[]{:S(2)}) %collective-permute-start.7) | collective-permute-done | bytes 196640 | tf_op jit(solution)/shard_map/ppermute | solution.py:76
  51.4 18.3 %attend.1 = (bf16[1024,768]{1,0:T(8,128)(2,1)}, bf16[1024,768]{1,0:T(8,128)(2,1)}, bf16[1024,768]{1,0:T(8,128)(2,1)}, bf16[1024,768]{1,0:T(8,128)(2,1)}, f32[2,1...) custom-call(s32[5]{0:T(128)} %stack.29.pos, s32[2]{0:T(128)} %lengths.7, bf16[1024,768]{1,0:T(8,128)(2,1)} %bitcast.45, ...), custom_call_target="tpu_custom_call" | custom-call | flops 289910292480 | bytes 188743680 | tf_op jit(solution)/shard_map/attend/pallas_call | solution.py:49
  78.5 19.6 %expand.1 = (bf16[1024,3072]{1,0:T(8,128)(2,1)}, bf16[1024,3072]{1,0:T(8,128)(2,1)}, f32[1024,768]{1,0:T(8,128)}, f32[1024,128]{1,0:T(8,128)}, bf16[768,3072]{1,0:T(8,128)(2,1)}, /*index=5*/bf16[768,768]{1,0:T(8,128)(2,1)}) custom-call(s32[5]{0:T(128)} %stack.29.pos, bf16[1024,768]{1,0:T(8,128)(2,1)} %bitcast.46, ...), custom_call_target="tpu_custom_call" | custom-call | flops 193273528320 | bytes 283115520 | tf_op jit(solution)/shard_map/expand/pallas_call | solution.py:49
  102.2 48.8 %feed_forward.1 = (bf16[1024,768]{1,0:T(8,128)(2,1)}, f32[1024,768]{1,0:T(8,128)}, bf16[1024,768]{1,0:T(8,128)(2,1)}, bf16[4,4,192,384]{3,2,1,0:T(8,128)(2,1)}, ...) custom-call(s32[5]{0:T(128)} %stack.29.pos, s32[2]{0:T(128)} %lengths.7, ...), custom_call_target="tpu_custom_call" | custom-call | flops 531502202880 | bytes 786432000 | tf_op jit(solution)/shard_map/feed_forward/pallas_call | solution.py:49
  151.3 4.7 %collective-permute-done.28.got = bf16[4,4,192,384]{3,2,1,0:T(8,128)(2,1)} collective-permute-done((bf16[4,4,192,384]{3,2,1,0:T(8,128)(2,1)}, bf16[4,4,192,384]{3,2,1,0:T(8,128)(2,1)}, u32[]{:S(2)}, u32[]{:S(2)}) %collective-permute-start.28) | collective-permute-done | bytes 2359328 | tf_op jit(solution)/shard_map/ppermute | solution.py:71
  156.2 4.2 %add_first.3 = (bf16[2,2,192,384]{3,2,1,0:T(8,128)(2,1)}, bf16[2,2,192,384]{3,2,1,0:T(8,128)(2,1)}, bf16[2,2,192,384]{3,2,1,0:T(8,128)(2,1)}, bf16[2,2,192,384]{3,2,1,0:T(8,128)(2,1)}) custom-call(s32[5]{0:T(128)} %stack.29.pos, bf16[4,4,192,384]{3,2,1,0:T(8,128)(2,1)} %get-tuple-element.210.keep, bf16[4,4,192,384]{3,2,1,0:T(8,128)(2,1)} %collective-permute-done.28.got), custom_call_target="tpu_custom_call" | custom-call | bytes 141557760 | tf_op jit(solution)/shard_map/add_first/pallas_call | solution.py:49
  162.3 5.2 %add_first.4 = (bf16[2,2,256,384]{3,2,1,0:T(8,128)(2,1)}, bf16[2,2,256,384]{3,2,1,0:T(8,128)(2,1)}, bf16[2,2,256,384]{3,2,1,0:T(8,128)(2,1)}, bf16[2,2,256,384]{3,2,1,0:T(8,128)(2,1)}) custom-call(s32[5]{0:T(128)} %stack.29.pos, bf16[4,4,256,384]{3,2,1,0:T(8,128)(2,1)} %get-tuple-element.220.keep, bf16[4,4,256,384]{3,2,1,0:T(8,128)(2,1)} %collective-permute-done.31.got), custom_call_target="tpu_custom_call" | custom-call | bytes 188743680 | tf_op jit(solution)/shard_map/add_first/pallas_call | solution.py:49
  169.8 14.1 %pair_back.2 = (bf16[1024,2304]{1,0:T(8,128)(2,1)}, f32[8,768]{1,0:T(8,128)}) custom-call(s32[2]{0:T(128)} %lengths.7, bf16[1024,768]{1,0:T(8,128)(2,1)} %get-tuple-element.215.q, bf16[1024,768]{1,0:T(8,128)(2,1)} %get-tuple-element.216.k, bf16[1024,768]{1,0:T(8,128)(2,1)} %get-tuple-element.217.v, bf16[1024,768]{1,0:T(8,128)(2,1)} %get-tuple-element.192.mixed, ...), custom_call_target="tpu_custom_call" | custom-call | flops 144955146240 | bytes 188743680 | tf_op jit(solution)/shard_map/pair_back/pallas_call | solution.py:49
  183.9 2.8 add_second.3
  188.6 14.3 %pair_back.3 = (bf16[1024,2304]{1,0:T(8,128)(2,1)}, f32[8,768]{1,0:T(8,128)}) custom-call(s32[2]{0:T(128)} %lengths.7, bf16[1024,768]{1,0:T(8,128)(2,1)} %get-tuple-element.215.q, bf16[1024,768]{1,0:T(8,128)(2,1)} %get-tuple-element.216.k, bf16[1024,768]{1,0:T(8,128)(2,1)} %get-tuple-element.217.v, ...), custom_call_target="tpu_custom_call", output_to_operand_aliasing={{0}: (8, {})} | custom-call | flops 144955146240 | bytes 188743680 | tf_op jit(solution)/shard_map/pair_back/pallas_call | solution.py:49
  203.0 3.2 %add_second.4 = (bf16[2,256,384]{2,1,0:T(8,128)(2,1)}, bf16[2,256,384]{2,1,0:T(8,128)(2,1)}, bf16[2,256,384]{2,1,0:T(8,128)(2,1)}, bf16[2,256,384]{2,1,0:T(8,128)(2,1)}) custom-call(s32[5]{0:T(128)} %stack.29.pos, bf16[2,2,256,384]{3,2,1,0:T(8,128)(2,1)} %get-tuple-element.224.ka, bf16[2,2,256,384]{3,2,1,0:T(8,128)(2,1)} %collective-permute-done.34.ra, ...), custom_call_target="tpu_custom_call" | custom-call | bytes 94371840 | tf_op jit(solution)/shard_map/add_second/pallas_call | solution.py:49
  215.0 10.2 %heads_weights.1 = (bf16[4,4,160,384]{3,2,1,0:T(8,128)(2,1)}, bf16[4,4,160,384]{3,2,1,0:T(8,128)(2,1)}) custom-call(s32[5]{0:T(128)} %stack.29.pos, bf16[1024,768]{1,0:T(8,128)(2,1)} %bitcast.47, bf16[1024,2304]{1,0:T(8,128)(2,1)} %get-tuple-element.237.grads, f32[8,768]{1,0:T(8,128)} %get-tuple-element.247.sums), custom_call_target="tpu_custom_call" | custom-call | flops 72477573120 | bytes 188743680 | tf_op jit(solution)/shard_map/heads_weights/pallas_call | solution.py:49
  226.2 2.4 add_third.4
  233.0 3.7 %add_first.5 = (bf16[2,2,160,384]{3,2,1,0:T(8,128)(2,1)}, bf16[2,2,160,384]{3,2,1,0:T(8,128)(2,1)}, bf16[2,2,160,384]{3,2,1,0:T(8,128)(2,1)}, bf16[2,2,160,384]{3,2,1,0:T(8,128)(2,1)}) custom-call(s32[5]{0:T(128)} %stack.29.pos, bf16[4,4,160,384]{3,2,1,0:T(8,128)(2,1)} %get-tuple-element.248.keep, bf16[4,4,160,384]{3,2,1,0:T(8,128)(2,1)} %collective-permute-done.41.got), custom_call_target="tpu_custom_call" | custom-call | bytes 117964800 | tf_op jit(solution)/shard_map/add_first/pallas_call | solution.py:49
  238.7 8.8 %inputs_back.1 = bf16[1024,768]{1,0:T(8,128)(2,1)} custom-call(f32[1024,768]{1,0:T(8,128)} %get-tuple-element.262.grad_first, bf16[1024,2304]{1,0:T(8,128)(2,1)} %get-tuple-element.237.grads, bf16[768,2304]{1,0:T(8,128)(2,1)} %get-tuple-element.188.weight), custom_call_target="tpu_custom_call" | custom-call | flops 72477573120 | bytes 251658240 | tf_op jit(solution)/shard_map/inputs_back/pallas_call | solution.py:49
  250.1 2.6 add_second.5
  279.0 2.5 join.5.mine
  287.5 4.6 %place_ffn.1 = (f32[768,768]{1,0:T(8,128)}, f32[192,3072]{1,0:T(8,128)}, f32[192,768]{1,0:T(8,128)}, f32[1,192]{1,0:T(1,128)}, f32[1,192]{1,0:T(1,128)}, /*index...) custom-call(s32[5]{0:T(128)} %stack.29.pos, ...), custom_call_target="tpu_custom_call" | custom-call | bytes 70778880 | tf_op jit(solution)/shard_map/place_ffn/pallas_call | solution.py:49
  295.7 2.6 place_heads.1
  (237 shorter events, 99.3 us)
Async XLA Ops:
  21.6 22.4 %collective-permute-start = (bf16[192,384]{1,0:T(8,128)(2,1)}, bf16[192,384]{1,0:T(8,128)(2,1)S(1)}, u32[]{:S(2)}, u32[]{:S(2)}) collective-permute-start(bf16[192,384]{1,0:T(8,128)(2,1)} %get-tuple-element.186), channel_id=1, source_target_pairs={{0,8},{8,0},{16,24},{24,16},{1,9},{9,1},{17,25},{25,17},{2,10},{10... | collective-permute-start | bytes 442376 | tf_op jit(solution)/shard_map/ppermute | solution.py:76
  24.0 17.1 %collective-permute-start.7 = (bf16[256,384]{1,0:T(8,128)(2,1)}, bf16[256,384]{1,0:T(8,128)(2,1)S(1)}, u32[]{:S(2)}, u32[]{:S(2)}) collective-permute-start(bf16[256,384]{1,0:T(8,128)(2,1)} %cut_more.1), channel_id=1, source_target_pairs={{0,16},{8,24},{16,0},{24,8},{1,17},{9,25},{17,1},{25,9},{2,18},{10... | collective-permute-start | bytes 589832 | tf_op jit(solution)/shard_map/ppermute | solution.py:76
  34.9 15.1 %collective-permute-start.16 = (bf16[1728,384]{1,0:T(8,128)(2,1)S(1)}, bf16[1728,384]{1,0:T(8,128)(2,1)}, u32[]{:S(2)}, u32[]{:S(2)}) collective-permute-start(bf16[1728,384]{1,0:T(8,128)(2,1)S(1)} %constant_dynamic-update-slice_fusion.3.rest_0_), channel_id=1, source_target_pairs={{0,1},{1,0},{2,3},{3,2},{4,5},{5,4},{6,7},{7,6},{8,9},{9,8},{10,11... | collective-permute-start | bytes 3981320 | tf_op jit(solution)/shard_map/ppermute | solution.py:71
  44.0 25.7 %collective-permute-start.15 = (bf16[192,384]{1,0:T(8,128)(2,1)}, bf16[192,384]{1,0:T(8,128)(2,1)}, u32[]{:S(2)}, u32[]{:S(2)}) collective-permute-start(bf16[192,384]{1,0:T(8,128)(2,1)} %get-tuple-element.186), channel_id=1, source_target_pairs={{0,24},{8,16},{16,8},{24,0},{1,25},{9,17},{17,9},{25,1},{2,26},{10... | collective-permute-start | bytes 442376 | tf_op jit(solution)/shard_map/ppermute | solution.py:76
  46.2 23.5 %collective-permute-start.14 = (bf16[192,384]{1,0:T(8,128)(2,1)}, bf16[192,384]{1,0:T(8,128)(2,1)}, u32[]{:S(2)}, u32[]{:S(2)}) collective-permute-start(bf16[192,384]{1,0:T(8,128)(2,1)} %get-tuple-element.186), channel_id=1, source_target_pairs={{0,16},{8,24},{16,0},{24,8},{1,17},{9,25},{17,1},{25,9},{2,18},{10... | collective-permute-start | bytes 442376 | tf_op jit(solution)/shard_map/ppermute | solution.py:76
  46.2 23.5 %collective-permute-start.13 = (bf16[720,384]{1,0:T(8,128)(2,1)}, bf16[720,384]{1,0:T(8,128)(2,1)}, u32[]{:S(2)}, u32[]{:S(2)}) collective-permute-start(bf16[720,384]{1,0:T(8,128)(2,1)} %pad_maximum_fusion.rest_0_), channel_id=1, source_target_pairs={{0,6},{1,7},{2,4},{3,5},{4,2},{5,3},{6,0},{7,1},{8,14},{9,15},{10,... | collective-permute-start | bytes 1658888 | tf_op jit(solution)/shard_map/ppermute | solution.py:71
  47.2 22.9 %collective-permute-start.12 = (bf16[720,384]{1,0:T(8,128)(2,1)}, bf16[720,384]{1,0:T(8,128)(2,1)}, u32[]{:S(2)}, u32[]{:S(2)}) collective-permute-start(bf16[720,384]{1,0:T(8,128)(2,1)} %pad_maximum_fusion.rest_0_), channel_id=1, source_target_pairs={{0,4},{1,5},{2,6},{3,7},{4,0},{5,1},{6,2},{7,3},{8,12},{9,13},{10,... | collective-permute-start | bytes 1658888 | tf_op jit(solution)/shard_map/ppermute | solution.py:71
  50.0 21.4 %collective-permute-start.11 = (bf16[720,384]{1,0:T(8,128)(2,1)}, bf16[720,384]{1,0:T(8,128)(2,1)}, u32[]{:S(2)}, u32[]{:S(2)}) collective-permute-start(bf16[720,384]{1,0:T(8,128)(2,1)} %pad_maximum_fusion.rest_0_), channel_id=1, source_target_pairs={{0,2},{1,3},{2,0},{3,1},{4,6},{5,7},{6,4},{7,5},{8,10},{9,11},{10,... | collective-permute-start | bytes 1658888 | tf_op jit(solution)/shard_map/ppermute | solution.py:71
  74.9 23.2 %collective-permute-start.24 = (bf16[576,384]{1,0:T(8,128)(2,1)}, bf16[576,384]{1,0:T(8,128)(2,1)}, u32[]{:S(2)}, u32[]{:S(2)}) collective-permute-start(bf16[576,384]{1,0:T(8,128)(2,1)} %join.3.rest_0_), channel_id=1, source_target_pairs={{0,1},{1,0},{2,3},{3,2},{4,5},{5,4},{6,7},{7,6},{8,9},{9,8},{10,11... | collective-permute-start | bytes 1327112 | tf_op jit(solution)/shard_map/ppermute | solution.py:71
  74.9 23.2 %collective-permute-start.23 = (bf16[576,384]{1,0:T(8,128)(2,1)}, bf16[576,384]{1,0:T(8,128)(2,1)}, u32[]{:S(2)}, u32[]{:S(2)}) collective-permute-start(bf16[576,384]{1,0:T(8,128)(2,1)} %join.3.rest_0_), channel_id=1, source_target_pairs={{0,6},{1,7},{2,4},{3,5},{4,2},{5,3},{6,0},{7,1},{8,14},{9,15},{10,... | collective-permute-start | bytes 1327112 | tf_op jit(solution)/shard_map/ppermute | solution.py:71
  76.3 21.9 %collective-permute-start.22 = (bf16[576,384]{1,0:T(8,128)(2,1)}, bf16[576,384]{1,0:T(8,128)(2,1)}, u32[]{:S(2)}, u32[]{:S(2)}) collective-permute-start(bf16[576,384]{1,0:T(8,128)(2,1)} %join.3.rest_0_), channel_id=1, source_target_pairs={{0,4},{1,5},{2,6},{3,7},{4,0},{5,1},{6,2},{7,3},{8,12},{9,13},{10,... | collective-permute-start | bytes 1327112 | tf_op jit(solution)/shard_map/ppermute | solution.py:71
  76.9 21.3 %collective-permute-start.21 = (bf16[576,384]{1,0:T(8,128)(2,1)}, bf16[576,384]{1,0:T(8,128)(2,1)}, u32[]{:S(2)}, u32[]{:S(2)}) collective-permute-start(bf16[576,384]{1,0:T(8,128)(2,1)} %join.3.rest_0_), channel_id=1, source_target_pairs={{0,2},{1,3},{2,0},{3,1},{4,6},{5,7},{6,4},{7,5},{8,10},{9,11},{10,... | collective-permute-start | bytes 1327112 | tf_op jit(solution)/shard_map/ppermute | solution.py:71
  160.3 23.5 %collective-permute-start.29 = (bf16[2,2,192,384]{3,2,1,0:T(8,128)(2,1)}, bf16[2,2,192,384]{3,2,1,0:T(8,128)(2,1)}, u32[]{:S(2)}, u32[]{:S(2)}) collective-permute-start(bf16[2,2,192,384]{3,2,1,0:T(8,128)(2,1)} %get-tuple-element.213), channel_id=1, source_target_pairs={{0,2},{1,3},{2,0},{3,1},{4,6},{5,7},{6,4},{7,5},{8,10},{9,11},{10,... | collective-permute-start | bytes 1769480 | tf_op jit(solution)/shard_map/ppermute | solution.py:71
  160.9 23.0 %collective-permute-start.30 = (bf16[2,2,192,384]{3,2,1,0:T(8,128)(2,1)}, bf16[2,2,192,384]{3,2,1,0:T(8,128)(2,1)}, u32[]{:S(2)}, u32[]{:S(2)}) collective-permute-start(bf16[2,2,192,384]{3,2,1,0:T(8,128)(2,1)} %get-tuple-element.214), channel_id=1, source_target_pairs={{0,4},{1,5},{2,6},{3,7},{4,0},{5,1},{6,2},{7,3},{8,12},{9,13},{10,... | collective-permute-start | bytes 1769480 | tf_op jit(solution)/shard_map/ppermute | solution.py:71
  167.6 35.4 %collective-permute-start.34 = (bf16[2,2,256,384]{3,2,1,0:T(8,128)(2,1)}, bf16[2,2,256,384]{3,2,1,0:T(8,128)(2,1)}, u32[]{:S(2)}, u32[]{:S(2)}) collective-permute-start(bf16[2,2,256,384]{3,2,1,0:T(8,128)(2,1)} %get-tuple-element.233), channel_id=1, source_target_pairs={{0,2},{1,3},{2,0},{3,1},{4,6},{5,7},{6,4},{7,5},{8,10},{9,11},{10,... | collective-permute-start | bytes 2359304 | tf_op jit(solution)/shard_map/ppermute | solution.py:71
  168.4 34.6 %collective-permute-start.35 = (bf16[2,2,256,384]{3,2,1,0:T(8,128)(2,1)}, bf16[2,2,256,384]{3,2,1,0:T(8,128)(2,1)}, u32[]{:S(2)}, u32[]{:S(2)}) collective-permute-start(bf16[2,2,256,384]{3,2,1,0:T(8,128)(2,1)} %get-tuple-element.234), channel_id=1, source_target_pairs={{0,4},{1,5},{2,6},{3,7},{4,0},{5,1},{6,2},{7,3},{8,12},{9,13},{10,... | collective-permute-start | bytes 2359304 | tf_op jit(solution)/shard_map/ppermute | solution.py:71
  186.7 19.5 %collective-permute-start.32 = (bf16[2,192,384]{2,1,0:T(8,128)(2,1)}, bf16[2,192,384]{2,1,0:T(8,128)(2,1)}, u32[]{:S(2)}, u32[]{:S(2)}) collective-permute-start(bf16[2,192,384]{2,1,0:T(8,128)(2,1)} %get-tuple-element.231), channel_id=1, source_target_pairs={{0,4},{1,5},{2,6},{3,7},{4,0},{5,1},{6,2},{7,3},{8,12},{9,13},{10,... | collective-permute-start | bytes 884744 | tf_op jit(solution)/shard_map/ppermute | solution.py:71
  187.3 18.9 %collective-permute-start.33 = (bf16[2,192,384]{2,1,0:T(8,128)(2,1)}, bf16[2,192,384]{2,1,0:T(8,128)(2,1)}, u32[]{:S(2)}, u32[]{:S(2)}) collective-permute-start(bf16[2,192,384]{2,1,0:T(8,128)(2,1)} %get-tuple-element.232), channel_id=1, source_target_pairs={{0,2},{1,3},{2,0},{3,1},{4,6},{5,7},{6,4},{7,5},{8,10},{9,11},{10,... | collective-permute-start | bytes 884744 | tf_op jit(solution)/shard_map/ppermute | solution.py:71
  208.3 17.0 %collective-permute-start.38 = (bf16[192,384]{1,0:T(8,128)(2,1)}, bf16[192,384]{1,0:T(8,128)(2,1)S(1)}, u32[]{:S(2)}, u32[]{:S(2)}) collective-permute-start(bf16[192,384]{1,0:T(8,128)(2,1)} %get-tuple-element.252), channel_id=1, source_target_pairs={{0,8},{8,0},{16,24},{24,16},{1,9},{9,1},{17,25},{25,17},{2,10},{10... | collective-permute-start | bytes 442376 | tf_op jit(solution)/shard_map/ppermute | solution.py:76
  210.6 14.7 %collective-permute-start.39 = (bf16[192,384]{1,0:T(8,128)(2,1)}, bf16[192,384]{1,0:T(8,128)(2,1)}, u32[]{:S(2)}, u32[]{:S(2)}) collective-permute-start(bf16[192,384]{1,0:T(8,128)(2,1)} %get-tuple-element.253), channel_id=1, source_target_pairs={{0,16},{8,24},{16,0},{24,8},{1,17},{9,25},{17,1},{25,9},{2,18},{10... | collective-permute-start | bytes 442376 | tf_op jit(solution)/shard_map/ppermute | solution.py:76
  211.0 14.3 %collective-permute-start.40 = (bf16[192,384]{1,0:T(8,128)(2,1)}, bf16[192,384]{1,0:T(8,128)(2,1)}, u32[]{:S(2)}, u32[]{:S(2)}) collective-permute-start(bf16[192,384]{1,0:T(8,128)(2,1)} %get-tuple-element.254), channel_id=1, source_target_pairs={{0,24},{8,16},{16,8},{24,0},{1,25},{9,17},{17,9},{25,1},{2,26},{10... | collective-permute-start | bytes 442376 | tf_op jit(solution)/shard_map/ppermute | solution.py:76
  228.6 18.9 %collective-permute-start.44 = (bf16[256,384]{1,0:T(8,128)(2,1)}, bf16[256,384]{1,0:T(8,128)(2,1)}, u32[]{:S(2)}, u32[]{:S(2)}) collective-permute-start(bf16[256,384]{1,0:T(8,128)(2,1)} %get-tuple-element.265), channel_id=1, source_target_pairs={{0,8},{8,0},{16,24},{24,16},{1,9},{9,1},{17,25},{25,17},{2,10},{10... | collective-permute-start | bytes 589832 | tf_op jit(solution)/shard_map/ppermute | solution.py:76
  229.7 17.8 %collective-permute-start.45 = (bf16[256,384]{1,0:T(8,128)(2,1)}, bf16[256,384]{1,0:T(8,128)(2,1)}, u32[]{:S(2)}, u32[]{:S(2)}) collective-permute-start(bf16[256,384]{1,0:T(8,128)(2,1)} %get-tuple-element.266), channel_id=1, source_target_pairs={{0,16},{8,24},{16,0},{24,8},{1,17},{9,25},{17,1},{25,9},{2,18},{10... | collective-permute-start | bytes 589832 | tf_op jit(solution)/shard_map/ppermute | solution.py:76
  231.1 16.4 %collective-permute-start.46 = (bf16[256,384]{1,0:T(8,128)(2,1)}, bf16[256,384]{1,0:T(8,128)(2,1)}, u32[]{:S(2)}, u32[]{:S(2)}) collective-permute-start(bf16[256,384]{1,0:T(8,128)(2,1)} %get-tuple-element.267), channel_id=1, source_target_pairs={{0,24},{8,16},{16,8},{24,0},{1,25},{9,17},{17,9},{25,1},{2,26},{10... | collective-permute-start | bytes 589832 | tf_op jit(solution)/shard_map/ppermute | solution.py:76
  (76 other events, 515.3 us)
